TPU v7x, 512 devices: a whole 4x4x16 slice. The times are simulated.
512 devices in a mesh: ctx: 64 (over z_hi, x, y), ch: 8 (over z_lo, core).
Axes of the slice: x: 4, y: 4, z: 16 (z_hi: 4, z_lo: 4; z = z_hi * 4 + z_lo), core: 2. Of those that a mesh axis runs over, the one named last changes fastest.
Arguments:
- features: bfloat16 [8192, 8192], P('ctx', 'ch'), as said below
- norm_gain: float32 [8192], P('ch'), may hold values from 0.5 to 1.5
- skip_gain: float32 [8192], P('ch'), may hold values from -1 to 1
- gate_value: bfloat16 [8192, 8192], P('ctx', 'ch'), may hold values from -6 to 6
- cotangent: bfloat16 [8192, 8192], P('ctx', 'ch'), may hold values from -6 to 6
- residue: float32 [512, 16], P('ch'), as said below
- log_rate: float32 [512, 16], P('ch'), as said below
Outputs:
- gated_out: bfloat16 [8192, 8192], P('ctx', 'ch')
- grad_residue: float32 [512, 16], P('ch')
- grad_log_rate: float32 [512, 16], P('ch')
Inputs may be any that keep to these rules, and one draw needn't show every extreme that they name: `features`: Real-valued activations. `residue`: Real-valued mode weights. exp(log_rate) lies between 0.25 / 8192 and 0.125.
All inputs are finite; a program needn't handle non-finite values.
Results may differ from a plain program's by a relative error of at most 0.0057.
Values may be sent and summed in bfloat16 or wider, within the bound.
A program may use at most 64 MiB of HBM per device.

v0:
```python
import math

import jax
import jax.numpy as jnp
from jax import lax
from jax.sharding import PartitionSpec as P

EPSILON = 1e-06
HIGHEST = lax.Precision.HIGHEST
HIGHER = lax.Precision.HIGH


def chain_modes(earlier, later_part):
    decay_a, length_a, state_a, second_a = earlier
    decay_b, length_b, state_b, second_b = later_part
    return (
        decay_a * decay_b,
        length_a + length_b,
        decay_b * state_a + state_b,
        decay_b * (second_a + length_b * state_a) + second_b,
    )


def as_items(values, block_len, group_size):
    row_count, chan_count = values.shape
    blocks = values.reshape(row_count // block_len, block_len, chan_count // group_size, group_size)
    return blocks.transpose(0, 2, 3, 1).reshape(-1, group_size, block_len)


def from_items(item_rows, block_count, filter_count):
    item_total, group_size, block_len = item_rows.shape
    blocks = item_rows.reshape(block_count, filter_count, group_size, block_len).transpose(
        0, 3, 1, 2
    )
    return blocks.reshape(block_count * block_len, filter_count * group_size)


def spanned(function, arrays, batch_width):
    item_total = arrays[0].shape[0]
    piece_size = math.gcd(item_total, batch_width)
    folded = tuple(
        (
            member.reshape((item_total // piece_size, piece_size) + member.shape[1:])
            for member in arrays
        )
    )
    result = lax.map(function, folded)
    return tuple((member.reshape((item_total,) + member.shape[2:]) for member in result))


def summarize(packed):
    x_part, rate_vals = packed
    x_float = x_part.astype(jnp.float32)
    block_len = x_part.shape[2]
    back_dist = block_len - 1.0 - jnp.arange(block_len, dtype=jnp.float32)
    weights = jnp.exp(-rate_vals[:, :, None] * back_dist)
    first_sum = jnp.einsum("cms,cgs->cmg", weights, x_float, precision=HIGHER)
    second_sum = jnp.einsum("cms,cgs->cmg", weights * back_dist, x_float, precision=HIGHER)
    return (first_sum, second_sum)


def block_terms(packed):
    x_part, d_part, rate_vals, residues, skip_vals, state_one, state_two = packed
    x_float = x_part.astype(jnp.float32)
    d_float = d_part.astype(jnp.float32)
    block_len = x_part.shape[2]
    places = jnp.arange(block_len, dtype=jnp.float32)
    middle = (block_len - 1) / 2.0
    falling = jnp.exp(-rate_vals[:, :, None] * (places - middle))
    rising = jnp.exp(rate_vals[:, :, None] * (places - middle))
    after_decay = jnp.exp(-rate_vals[:, :, None] * (places + 1.0))
    lag_grid = places[:, None] - places[None, :]
    causal = lag_grid >= 0
    kernel = jnp.einsum("cmt,cms->cts", residues[:, :, None] * falling, rising, precision=HIGHEST)
    kernel = jnp.where(causal, kernel, 0.0)
    output = jnp.einsum("cts,cgs->cgt", kernel, x_float, precision=HIGHER)
    output = output + jnp.einsum(
        "cmt,cmg->cgt", residues[:, :, None] * after_decay, state_one, precision=HIGHEST
    )
    output = output + skip_vals[:, :, None] * x_float
    paired = jnp.einsum("cgt,cgs->cts", d_part, x_part, preferred_element_type=jnp.float32)
    paired = jnp.where(causal, paired, 0.0)
    near_sum = jnp.einsum("cts,cms->cmt", paired, rising, precision=HIGHEST)
    lag_sum = jnp.einsum("cts,cms->cmt", paired * lag_grid, rising, precision=HIGHEST)
    local_one = jnp.sum(near_sum * falling, axis=2)
    local_two = jnp.sum(lag_sum * falling, axis=2)
    carried = jnp.einsum("cmt,cgt->cmg", after_decay, d_float, precision=HIGHER)
    carried_lag = jnp.einsum(
        "cmt,cgt->cmg", after_decay * (places + 1.0), d_float, precision=HIGHER
    )
    grad_one = local_one + jnp.sum(state_one * carried, axis=2)
    grad_two = local_two + jnp.sum(state_one * carried_lag + state_two * carried, axis=2)
    return (output, grad_one, grad_two)


def mixer(x_norm, d_norm, rate_vals, residues, skip_vals, block_len):
    row_count, chan_count = x_norm.shape
    filter_count, mode_count = rate_vals.shape
    group_size = chan_count // filter_count
    block_count = row_count // block_len
    x_items = as_items(x_norm, block_len, group_size)
    d_items = as_items(d_norm, block_len, group_size)
    rate_items = jnp.tile(rate_vals, (block_count, 1))
    residue_items = jnp.tile(residues, (block_count, 1))
    skip_items = jnp.tile(skip_vals.reshape(filter_count, group_size), (block_count, 1))
    first_sum, second_sum = spanned(summarize, (x_items, rate_items), 8)
    first_sum = first_sum.reshape(block_count, filter_count, mode_count, group_size)
    second_sum = second_sum.reshape(block_count, filter_count, mode_count, group_size)
    decays = jnp.broadcast_to(
        jnp.exp(-rate_vals * block_len)[None, :, :, None],
        (block_count, filter_count, mode_count, 1),
    )
    lengths = jnp.full((block_count, filter_count, mode_count, 1), float(block_len), jnp.float32)
    inclusive = lax.associative_scan(chain_modes, (decays, lengths, first_sum, second_sum), axis=0)
    opening = (
        jnp.ones((1, filter_count, mode_count, 1), jnp.float32),
        jnp.zeros((1, filter_count, mode_count, 1), jnp.float32),
        jnp.zeros((1, filter_count, mode_count, group_size), jnp.float32),
        jnp.zeros((1, filter_count, mode_count, group_size), jnp.float32),
    )
    exclusive = tuple(
        (
            jnp.concatenate([head_part, member[:-1]], axis=0)
            for head_part, member in zip(opening, inclusive)
        )
    )
    state_one = exclusive[2].reshape(block_count * filter_count, mode_count, group_size)
    state_two = exclusive[3].reshape(block_count * filter_count, mode_count, group_size)
    output, grad_one, grad_two = spanned(
        block_terms,
        (x_items, d_items, rate_items, residue_items, skip_items, state_one, state_two),
        8,
    )
    conv_out = from_items(output, block_count, filter_count).astype(jnp.bfloat16)
    grad_one = grad_one.reshape(block_count, filter_count, mode_count).sum(axis=0)
    grad_two = grad_two.reshape(block_count, filter_count, mode_count).sum(axis=0)
    return (conv_out, grad_one, grad_two)


def normalize(features, norm_gain):
    x_float = features.astype(jnp.float32)
    part_sum = jnp.sum(x_float * x_float, axis=1)
    total_sq = lax.psum(part_sum, "ch")
    mean_sq = total_sq / (features.shape[1] * lax.axis_size("ch"))
    scaled = x_float * lax.rsqrt(mean_sq + EPSILON)[:, None] * norm_gain[None, :]
    return scaled.astype(jnp.bfloat16)


def local(features, norm_gain, skip_gain, gate_value, cotangent, residue, log_rate):
    x_norm = normalize(features, norm_gain)
    d_norm = (cotangent.astype(jnp.float32) * gate_value.astype(jnp.float32)).astype(jnp.bfloat16)
    rate_vals = jnp.exp(log_rate)
    row_count = features.shape[0]
    ctx_count = lax.axis_size("ctx")
    seq_len = row_count * ctx_count
    moved_x, moved_d = (
        lax.all_to_all(x_norm, "ctx", split_axis=1, concat_axis=0, tiled=True),
        lax.all_to_all(d_norm, "ctx", split_axis=1, concat_axis=0, tiled=True),
    )
    ctx_index = lax.axis_index("ctx")
    local_chan = features.shape[1] // ctx_count
    local_filt = rate_vals.shape[0] // ctx_count
    rate_local = lax.dynamic_slice_in_dim(rate_vals, ctx_index * local_filt, local_filt, 0)
    res_local = lax.dynamic_slice_in_dim(residue, ctx_index * local_filt, local_filt, 0)
    skip_local = lax.dynamic_slice_in_dim(skip_gain, ctx_index * local_chan, local_chan, 0)
    local_out, grad_one, grad_two = mixer(
        moved_x, moved_d, rate_local, res_local, skip_local, min(256, seq_len)
    )
    conv_out = lax.all_to_all(local_out, "ctx", split_axis=0, concat_axis=1, tiled=True)
    pieces = (grad_one / seq_len, -res_local * rate_local * grad_two / seq_len)
    grad_res, grad_rate = (
        lax.all_gather(pieces[0], "ctx", axis=0, tiled=True),
        lax.all_gather(pieces[1], "ctx", axis=0, tiled=True),
    )
    gated_out = (gate_value.astype(jnp.float32) * conv_out.astype(jnp.float32)).astype(jnp.bfloat16)
    return (gated_out, grad_res, grad_rate)


def solution(mesh):
    in_specs = (
        P("ctx", "ch"),
        P("ch"),
        P("ch"),
        P("ctx", "ch"),
        P("ctx", "ch"),
        P("ch", None),
        P("ch", None),
    )
    out_specs = (P("ctx", "ch"), P("ch", None), P("ch", None))
    return jax.shard_map(local, mesh=mesh, in_specs=in_specs, out_specs=out_specs, check_vma=False)
```

profile of v0, /device:TPU:8, one launch (start us, length us, event | category | flops | bytes accessed | tf_op | source)
XLA Modules:
  0.0 569.3 jit_solution(15354232152159823896)
XLA Ops:
  2.0 17.6 %psum.7 = f32[128]{0:T(128)S(1)} all-reduce(f32[128]{0:T(128)S(1)} %fusion.90), channel_id=1, replica_groups=mesh['ctx'=64,'ch'=8] {'ch'}, use_global_device_ids=true, to_apply=%region_1.0 | all-reduce | flops 128 | bytes 1024 | tf_op jit(solution)/shard_map/psum | solution.py:143
  19.6 1.6 fusion.92
  21.2 18.5 %all-to-all-start = ((bf16[128,64,16]{0,2,1:T(8,128)(2,1)}), bf16[128,64,16]{0,2,1:T(8,128)(2,1)S(1)}, u32[]{:S(2)}, u32[]{:S(2)}) async-start(bf16[128,64,16]{0,2,1:T(8,128)(2,1)} %bitcast.14), calls=%async_computation | async-start | bytes 524288 | tf_op jit(solution)/shard_map/all_to_all | solution.py:157
  42.9 16.0 %all-to-all-done = bf16[128,64,16]{0,2,1:T(8,128)(2,1)S(1)} async-done(((bf16[128,64,16]{0,2,1:T(8,128)(2,1)}), bf16[128,64,16]{0,2,1:T(8,128)(2,1)S(1)}, u32[]{:S(2)}, u32[]{:S(2)}) %all-to-all-start) | async-done | bytes 262176 | tf_op jit(solution)/shard_map/all_to_all | solution.py:157
  58.9 9.3 %all-to-all-start.1 = ((bf16[128,64,16]{0,2,1:T(8,128)(2,1)}), bf16[128,64,16]{0,2,1:T(8,128)(2,1)S(1)}, u32[]{:S(2)}, u32[]{:S(2)}) async-start(bf16[128,64,16]{0,2,1:T(8,128)(2,1)} %bitcast.21), calls=%async_computation.1 | async-start | bytes 524288 | tf_op jit(solution)/shard_map/all_to_all | solution.py:158
  68.5 2.2 while.28
  73.4 13.1 %all-to-all-done.1 = bf16[128,64,16]{0,2,1:T(8,128)(2,1)S(1)} async-done(((bf16[128,64,16]{0,2,1:T(8,128)(2,1)}), bf16[128,64,16]{0,2,1:T(8,128)(2,1)S(1)}, u32[]{:S(2)}, u32[]{:S(2)}) %all-to-all-start.1) | async-done | bytes 262176 | tf_op jit(solution)/shard_map/all_to_all | solution.py:158
  86.7 32.4 %while.29 = (s32[]{:T(128)}, bf16[4,8,16,256]{3,2,1,0:T(8,128)(2,1)S(1)}, f32[4,8,16]{2,1,0:T(8,128)S(1)}, f32[4,8,16]{2,1,0:T(8,128)S(1)}, bf16[4,8,16,256]{3,2...) while((s32[]{:T(128)}, ...), condition=%wide.region_9.10_spmd, body=%wide.region_4.9_spmd.sunk | while | flops 384643456 | bytes 12352661 | solution.py:47
  87.4 1.9 fusion.153
  89.3 1.9 fusion.156
  91.8 2.0 fusion.150
  95.5 1.9 fusion.153
  97.4 1.9 fusion.156
  99.9 2.0 fusion.150
  103.6 1.9 fusion.153
  105.5 1.9 fusion.156
  108.0 2.0 fusion.150
  111.7 1.9 fusion.153
  113.6 1.9 fusion.156
  116.1 2.0 fusion.150
  120.1 7.5 %all-to-all-start.2 = ((bf16[64,128,16]{1,2,0:T(8,128)(2,1)}), bf16[64,128,16]{1,2,0:T(8,128)(2,1)S(1)}, u32[]{:S(2)}, u32[]{:S(2)}) async-start(bf16[64,128,16]{1,2,0:T(8,128)(2,1)} %copy.106), calls=%async_computation.2 | async-start | bytes 524288 | tf_op jit(solution)/shard_map/all_to_all | solution.py:169
  127.6 1.3 dynamic-slice
  129.8 212.9 %all-gather.1 = f32[64,1,16]{2,1,0:T(1,128)S(1)} all-gather(f32[1,1,16]{2,1,0:T(1,128)S(1)} %bitcast.136), channel_id=1, replica_groups=mesh['ctx'=64,'ch'=8] {'ctx'}, dimensions={0}, use_global_device_ids=true | all-gather | bytes 4160 | tf_op jit(solution)/shard_map/all_gather | solution.py:173
  343.6 224.0 %all-reduce.22 = f32[1024]{0:T(1024)S(1)} all-reduce(f32[1024]{0:T(1024)S(1)} %multiply_dynamic-update-slice_fusion), channel_id=2, replica_groups=mesh['ctx'=64,'ch'=8] {'ctx'}, use_global_device_ids=true, to_apply=%add.22 | all-reduce | flops 1024 | bytes 8192
  (175 shorter events, 21.8 us)
Async XLA Ops:
  0.6 40.3 %copy-start = (bf16[128,1024]{1,0:T(8,128)(2,1)S(1)}, bf16[128,1024]{1,0:T(8,128)(2,1)}, u32[]{:S(2)}) copy-start(bf16[128,1024]{1,0:T(8,128)(2,1)} %param.15) | copy-start | bytes 786436
  0.6 41.2 %copy-start.2 = (f32[64,16]{0,1:T(8,128)S(1)}, f32[64,16]{0,1:T(8,128)}, u32[]{:S(2)}) copy-start(f32[64,16]{0,1:T(8,128)} %param.16) | copy-start | bytes 12292
  0.7 41.2 %copy-start.1 = (f32[64,16]{0,1:T(8,128)S(1)}, f32[64,16]{0,1:T(8,128)}, u32[]{:S(2)}) copy-start(f32[64,16]{0,1:T(8,128)} %param.17) | copy-start | bytes 12292
  21.2 37.7 %all-to-all-start = ((bf16[128,64,16]{0,2,1:T(8,128)(2,1)}), bf16[128,64,16]{0,2,1:T(8,128)(2,1)S(1)}, u32[]{:S(2)}, u32[]{:S(2)}) async-start(bf16[128,64,16]{0,2,1:T(8,128)(2,1)} %bitcast.14), calls=%async_computation | async-start | bytes 524288 | tf_op jit(solution)/shard_map/all_to_all | solution.py:157
  58.9 27.6 %all-to-all-start.1 = ((bf16[128,64,16]{0,2,1:T(8,128)(2,1)}), bf16[128,64,16]{0,2,1:T(8,128)(2,1)S(1)}, u32[]{:S(2)}, u32[]{:S(2)}) async-start(bf16[128,64,16]{0,2,1:T(8,128)(2,1)} %bitcast.21), calls=%async_computation.1 | async-start | bytes 524288 | tf_op jit(solution)/shard_map/all_to_all | solution.py:158
  120.1 448.2 %all-to-all-start.2 = ((bf16[64,128,16]{1,2,0:T(8,128)(2,1)}), bf16[64,128,16]{1,2,0:T(8,128)(2,1)S(1)}, u32[]{:S(2)}, u32[]{:S(2)}) async-start(bf16[64,128,16]{1,2,0:T(8,128)(2,1)} %copy.106), calls=%async_computation.2 | async-start | bytes 524288 | tf_op jit(solution)/shard_map/all_to_all | solution.py:169
where the time goes:
time: 570 us; the launch traced here: 569 us
  blocking collectives  455 us (80%)
  starting transfers between devices  35.3 us (6%)
  matrix products  33.2 us (6%)
  waiting for transfers between devices  29.1 us (5%)
  local copies, waits for them, and re-layouts  10.3 us (2%)
    unnamed x1, blocking collectives  224 us
    all_gather x1, blocking collectives, local(): lax.all_gather(pieces[1], 'ctx', axis=0, tiled=True)  213 us
    all_to_all x1, starting transfers between devices, local(): lax.all_to_all(x_norm, 'ctx', split_axis=1, concat_axis=0, tiled=True)  18.5 us
    psum x1, blocking collectives, normalize(): total_sq = lax.psum(part_sum, 'ch')  17.6 us
    all_to_all x1, waiting for transfers between devices, local(): lax.all_to_all(x_norm, 'ctx', split_axis=1, concat_axis=0, tiled=True)  16 us
    all_to_all x1, waiting for transfers between devices, local(): lax.all_to_all(d_norm, 'ctx', split_axis=1, concat_axis=0, tiled=True)  13.1 us
  transfers between devices with their start and end apart: 3, of which 2 were waited for; matrix products, arithmetic and copies ran while one was open for 2% of the time, Pallas kernels for 0%

commit v1 on v0

v1 whole, which is shorter than its diff:
```python
import functools

import jax
import jax.numpy as jnp
from jax import lax
from jax.experimental import pallas as pl
from jax.experimental.pallas import tpu as pltpu
from jax.sharding import PartitionSpec as P

EPSILON = 1e-06
HIGHEST = lax.Precision.HIGHEST
F32 = jnp.float32
BF16 = jnp.bfloat16
LANES = 128
MODES = 16
GROUP = 16
PER_TILE = 8
MESH = pl.DeviceIdType.MESH


def iota(shape, axis):
    return lax.broadcasted_iota(jnp.int32, shape, axis)


def nt(a, b, precision=None):
    return lax.dot_general(
        a, b, (((1,), (1,)), ((), ())), precision=precision, preferred_element_type=F32
    )


def nn(a, b, precision=None):
    return lax.dot_general(
        a, b, (((1,), (0,)), ((), ())), precision=precision, preferred_element_type=F32
    )


def split(x):
    high = x.astype(BF16)
    low = (x - high.astype(F32)).astype(BF16)
    return jnp.concatenate([high, low], axis=1)


def own_filter(values):
    lane_filter = iota((MODES, LANES), 1) // GROUP
    kept = values[:MODES]
    for f in range(1, PER_TILE):
        kept = jnp.where(lane_filter == f, values[f * MODES : (f + 1) * MODES], kept)
    return kept


def body(
    plane, planes, groups, length,
    feat_hbm, gain_hbm, skip_hbm, gate_hbm, cot_hbm, res_hbm, lrate_hbm,
    out_ref, gres_ref, grate_ref,
    feat, gain, skip, gate, cot, res, lrate,
    xn, dn, rate_rows, res_rows, w_sum, a_out, decay, y_local, diag,
    sq_out, sq_in, s_out, s_in, c_out, c_in, l_out, l_in,
    z_out, z_in, zg_out, zg_in, r_out, r_in, g_out, g_in,
    pre_one,
    load_sem, send_sem, recv_sem,
):
    rows = feat.shape[0]
    tiles = feat.shape[1] // LANES
    ctx, ch = lax.axis_index("ctx"), lax.axis_index("ch")
    z_me, p_me = ctx // plane, ctx % plane

    loads = [
        pltpu.make_async_copy(src, dst, load_sem.at[n])
        for n, (src, dst) in enumerate(
            (
                (feat_hbm, feat), (lrate_hbm, lrate), (res_hbm, res), (gain_hbm, gain),
                (skip_hbm, skip), (cot_hbm, cot), (gate_hbm, gate),
            )
        )
    ]
    for load in loads:
        load.start()

    def plane_peer(i):
        return (p_me + i) % plane

    def z_peer(i):
        return (z_me + i) % planes

    barrier = pltpu.get_barrier_semaphore()
    for i in range(1, groups):
        pl.semaphore_signal(barrier, inc=1, device_id={"ch": (ch + i) % groups}, device_id_type=MESH)
    for i in range(1, plane):
        pl.semaphore_signal(
            barrier, inc=1, device_id={"ctx": z_me * plane + plane_peer(i)}, device_id_type=MESH
        )
    for i in range(1, planes):
        pl.semaphore_signal(
            barrier, inc=1, device_id={"ctx": z_peer(i) * plane + p_me}, device_id_type=MESH
        )

    def send_plane(src, dst, kind):
        for i in range(1, plane):
            peer = plane_peer(i)
            pltpu.make_async_remote_copy(
                src_ref=src.at[peer], dst_ref=dst.at[p_me],
                send_sem=send_sem.at[kind], recv_sem=recv_sem.at[kind],
                device_id={"ctx": z_me * plane + peer}, device_id_type=MESH,
            ).start()

    def send_z(src, dst, kind):
        for i in range(1, planes):
            pltpu.make_async_remote_copy(
                src_ref=src, dst_ref=dst.at[z_me],
                send_sem=send_sem.at[kind], recv_sem=recv_sem.at[kind],
                device_id={"ctx": z_peer(i) * plane + p_me}, device_id_type=MESH,
            ).start()

    def send_groups(src, dst, kind):
        for i in range(1, groups):
            pltpu.make_async_remote_copy(
                src_ref=src, dst_ref=dst.at[ch],
                send_sem=send_sem.at[kind], recv_sem=recv_sem.at[kind],
                device_id={"ch": (ch + i) % groups}, device_id_type=MESH,
            ).start()

    def wait_in(dst, kind):
        part = dst.at[pl.ds(0, dst.shape[0] - 1)]
        pltpu.make_async_copy(part, part, recv_sem.at[kind]).wait()

    def wait_out(dst, kind):
        part = dst.at[pl.ds(0, dst.shape[0] - 1)]
        pltpu.make_async_copy(part, part, send_sem.at[kind]).wait()

    loads[0].wait()
    squares = jnp.zeros((rows, LANES), F32)
    for j in range(tiles):
        part = feat[:, j * LANES : (j + 1) * LANES].astype(F32)
        squares += part * part
    sq_row = jnp.sum(jnp.transpose(squares), axis=0, keepdims=True)
    sq_out[...] = jnp.broadcast_to(sq_row, sq_out.shape)
    sq_in[ch] = sq_out[...]
    pl.semaphore_wait(barrier, (groups - 1) + (plane - 1) + (planes - 1))
    send_groups(sq_out, sq_in, 0)

    loads[1].wait()
    loads[2].wait()
    lanes_of_mode = (iota((MODES, LANES), 1) % MODES == iota((MODES, LANES), 0)).astype(F32)
    same_filter = iota((PER_TILE, LANES), 1) // MODES == iota((PER_TILE, LANES), 0)
    for j in range(tiles):
        part = slice(j * PER_TILE, (j + 1) * PER_TILE)
        rate_rep = nn(jnp.exp(lrate[part, :]), lanes_of_mode, HIGHEST)
        res_rep = nn(res[part, :], lanes_of_mode, HIGHEST)
        rate_row = jnp.sum(jnp.where(same_filter, rate_rep, 0.0), axis=0, keepdims=True)
        rate_rows[j] = jnp.broadcast_to(rate_row, (PER_TILE, LANES))
        res_rows[j] = jnp.where(same_filter, res_rep, 0.0)

    for n in range(3, 7):
        loads[n].wait()
    lane_up = iota((LANES, LANES), 1).astype(F32)
    row_up = iota((LANES, LANES), 0).astype(F32)

    def tables(j, carry):
        cols = pl.ds(pl.multiple_of(j * LANES, LANES), LANES)
        rate_wide = jnp.broadcast_to(rate_rows[j, 0:1, :], (LANES, LANES))
        rate_tall = jnp.transpose(rate_wide)
        back = (rows - 1.0) - lane_up
        weight = jnp.exp(-rate_tall * back)
        w_sum[j] = jnp.concatenate([split(weight), split(weight * back)], axis=0)
        res_wide = jnp.sum(res_rows[j], axis=0, keepdims=True)
        a_out[j] = split(res_wide * jnp.exp(-rate_wide * (row_up + 1.0)))
        mode_rate = own_filter(rate_tall)
        whole = jnp.exp(-mode_rate * float(rows))
        decay[2 * j] = whole[:8]
        decay[2 * j + 1] = whole[8:]
        d_part = (cot[:, cols].astype(F32) * gate[:, cols].astype(F32)).astype(BF16)
        dn[j] = d_part
        ahead = lane_up + 1.0
        after = jnp.exp(-rate_tall * ahead)
        both = jnp.concatenate([split(after), split(after * ahead)], axis=0)
        sums = nn(both, jnp.concatenate([d_part, d_part], axis=0))
        one, two = own_filter(sums[:LANES]), own_filter(sums[LANES:])
        for half in range(2):
            c_out[2 * j + half, 0:8] = one[8 * half : 8 * half + 8]
            c_out[2 * j + half, 8:16] = two[8 * half : 8 * half + 8]
        return carry

    lax.fori_loop(0, tiles, tables, 0)
    c_in[p_me] = c_out[p_me]
    send_plane(c_out, c_in, 1)

    wait_in(sq_in, 0)
    total_sq = sq_in[0]
    for n in range(1, groups):
        total_sq += sq_in[n]
    inverse = lax.rsqrt(total_sq / float(groups * tiles * LANES) + EPSILON)
    inverse = jnp.transpose(jnp.broadcast_to(inverse[0:1, :], (LANES, LANES)))

    def summaries(j, carry):
        cols = pl.ds(pl.multiple_of(j * LANES, LANES), LANES)
        x_part = (feat[:, cols].astype(F32) * inverse * gain[pl.ds(j, 1), :]).astype(BF16)
        xn[j] = x_part
        sums = nn(w_sum[j], jnp.concatenate([x_part, x_part], axis=0))
        one, two = own_filter(sums[:LANES]), own_filter(sums[LANES:])
        for half in range(2):
            s_out[2 * j + half, 0:8] = one[8 * half : 8 * half + 8]
            s_out[2 * j + half, 8:16] = two[8 * half : 8 * half + 8]
        return carry

    lax.fori_loop(0, tiles, summaries, 0)
    s_in[p_me] = s_out[p_me]
    send_plane(s_out, s_in, 2)

    lag = jnp.where(lane_up == 0.0, 0.0, rows - lane_up)
    lag_short = lag[:PER_TILE]
    lane_filter = iota((rows, LANES), 1) // GROUP
    short_lane, short_row = iota((8, LANES), 1), iota((8, LANES), 0)
    lane_mode = iota((MODES, LANES), 1) % MODES == iota((MODES, LANES), 0)

    def pairs(j, carry):
        x_part, d_part = xn[j], dn[j]
        lag_table = jnp.exp(-jnp.broadcast_to(rate_rows[j, 0:1, :], (LANES, LANES)) * jnp.where(row_up == 0.0, 0.0, rows - row_up))
        for f in range(PER_TILE):
            masked = jnp.where(lane_filter == f, d_part, jnp.zeros_like(d_part))
            product = nt(masked, x_part)
            total = None
            for i in range(rows // 8):
                piece = jnp.where(
                    short_lane <= short_row + 8 * i, product[8 * i : 8 * i + 8], 0.0
                )
                if i:
                    piece = pltpu.roll(piece, LANES - 8 * i, 1)
                total = piece if total is None else total + piece
            diag[f] = total
        near = None
        for u in range(8):
            piece = jnp.concatenate([diag[f, u : u + 1, :] for f in range(PER_TILE)], axis=0)
            if u:
                piece = pltpu.roll(piece, LANES - u, 1)
            near = piece if near is None else near + piece
        stacked = jnp.concatenate([near, near * lag_short], axis=0)
        local = nn(stacked, lag_table, HIGHEST)
        one = jnp.sum(jnp.where(same_filter, local[:8], 0.0), axis=0, keepdims=True)
        two = jnp.sum(jnp.where(same_filter, local[8:], 0.0), axis=0, keepdims=True)
        one = jnp.where(lane_mode, one, 0.0)
        two = jnp.where(lane_mode, two, 0.0)
        for half in range(2):
            l_out[2 * j + half, 0:8] = one[8 * half : 8 * half + 8]
            l_out[2 * j + half, 8:16] = two[8 * half : 8 * half + 8]
        return carry

    lax.fori_loop(0, tiles, pairs, 0)
    l_in[p_me] = l_out[p_me]
    send_plane(l_out, l_in, 3)

    wait_in(c_in, 1)
    wait_in(s_in, 2)
    step = decay[p_me]
    zero = jnp.zeros((8, LANES), F32)
    state, second, power = zero, zero, jnp.ones((8, LANES), F32)
    back_one, back_two, grad_one, grad_two = zero, zero, zero, zero
    for p in range(plane):
        sum_one, sum_two = s_in[p, 0:8], s_in[p, 8:16]
        cot_one, cot_two = c_in[p, 0:8], c_in[p, 8:16]
        pre_one[p] = state
        grad_one += state * cot_one
        grad_two += state * cot_two + second * cot_one
        back_one += power * cot_one
        back_two += power * (cot_two + float(rows * p) * cot_one)
        second = step * (second + float(rows) * state) + sum_two
        state = step * state + sum_one
        power = power * step
    z_out[...] = state
    z_in[z_me] = state
    send_z(z_out, z_in, 4)

    wait_in(l_in, 3)
    for p in range(plane):
        grad_one += l_in[p, 0:8]
        grad_two += l_in[p, 8:16]
    for n, value in enumerate((second, back_one, back_two, grad_one, grad_two)):
        zg_out[8 * n : 8 * n + 8] = value
    zg_in[z_me] = zg_out[...]
    send_z(zg_out, zg_in, 5)

    def inside(j, carry):
        x_part = xn[j]
        lag_table = jnp.exp(-jnp.broadcast_to(rate_rows[j, 0:1, :], (LANES, LANES)) * jnp.where(row_up == 0.0, 0.0, rows - row_up))
        filters = nt(res_rows[j], lag_table, HIGHEST)
        doubled = jnp.concatenate([x_part, x_part], axis=0)
        total = skip[pl.ds(j, 1), :] * x_part.astype(F32)
        for f in range(PER_TILE):
            first = pltpu.roll(
                jnp.broadcast_to(filters[f : f + 1], (8, LANES)), 0, 1, stride=1, stride_axis=0
            )
            pieces = []
            for i in range(rows // 8):
                piece = pltpu.roll(first, 8 * i, 1) if i else first
                pieces.append(jnp.where(short_lane <= short_row + 8 * i, piece, 0.0))
            toeplitz = split(jnp.concatenate(pieces, axis=0))
            total += jnp.where(lane_filter == f, nn(toeplitz, doubled), 0.0)
        y_local[j] = total
        return carry

    lax.fori_loop(0, tiles, inside, 0)

    wait_in(z_in, 4)
    plane_step = power
    entering = zero
    for z in range(planes - 1):
        entering = jnp.where(z_me > z, plane_step * entering + z_in[z], entering)
    power = jnp.ones((8, LANES), F32)
    for p in range(plane):
        r_out[p] = pre_one[p] + power * entering
        power = power * step
    r_in[p_me] = r_out[p_me]
    send_plane(r_out, r_in, 6)

    wait_in(zg_in, 5)
    grad_one, grad_two, state, second = zero, zero, zero, zero
    for z in range(planes):
        second_z, back_one, back_two, one, two = (zg_in[z, 8 * n : 8 * n + 8] for n in range(5))
        grad_one += one + state * back_one
        grad_two += two + state * back_two + second * back_one
        second = plane_step * (second + float(rows * plane) * state) + second_z
        state = plane_step * state + z_in[z]
    for p in range(plane):
        g_out[p, 0:8] = grad_one
        g_out[p, 8:16] = grad_two
    g_in[p_me] = g_out[p_me]
    send_plane(g_out, g_in, 7)

    wait_in(r_in, 6)
    own = iota((LANES, LANES), 1) // GROUP == iota((LANES, LANES), 0) // MODES

    def finish(j, carry):
        cols = pl.ds(pl.multiple_of(j * LANES, LANES), LANES)
        states = jnp.concatenate([r_in[2 * j], r_in[2 * j + 1]] * PER_TILE, axis=0)
        states = jnp.where(own, states, 0.0).astype(BF16)
        carried = nn(a_out[j], jnp.concatenate([states, states], axis=0))
        conv = (y_local[j] + carried).astype(BF16)
        out_ref[:, cols] = (gate[:, cols].astype(F32) * conv.astype(F32)).astype(BF16)
        return carry

    lax.fori_loop(0, tiles, finish, 0)

    wait_in(g_in, 7)
    same = same_filter.astype(F32)
    for j in range(tiles):
        part = slice(j * PER_TILE, (j + 1) * PER_TILE)
        stacked = jnp.concatenate(
            [g_in[2 * j, 0:8], g_in[2 * j + 1, 0:8], g_in[2 * j, 8:16], g_in[2 * j + 1, 8:16]],
            axis=0,
        )
        grads = nt(same, stacked, HIGHEST)
        gres_ref[part, :] = grads[:, :MODES] / float(length)
        grate_ref[part, :] = (
            -(res[part, :] * jnp.exp(lrate[part, :]) / float(length)) * grads[:, MODES:]
        )

    wait_out(sq_in, 0)
    for kind, buffer in ((1, c_in), (2, s_in), (3, l_in), (4, z_in), (5, zg_in), (6, r_in), (7, g_in)):
        wait_out(buffer, kind)


def solution(mesh):
    groups = mesh.shape["ch"]
    blocks = mesh.shape["ctx"]
    plane = 16
    planes = blocks // plane

    def local(features, norm_gain, skip_gain, gate_value, cotangent, residue, log_rate):
        rows, chans = features.shape
        tiles = chans // LANES
        filters = residue.shape[0]
        wide = lambda *shape: pltpu.VMEM(shape, F32)
        half = lambda *shape: pltpu.VMEM(shape, BF16)
        any_spec = pl.BlockSpec(memory_space=pl.ANY)
        vmem_spec = pl.BlockSpec(memory_space=pltpu.VMEM)
        return pl.pallas_call(
            functools.partial(body, plane, planes, groups, rows * blocks),
            out_shape=(
                jax.ShapeDtypeStruct((rows, chans), BF16),
                jax.ShapeDtypeStruct((filters, MODES), F32),
                jax.ShapeDtypeStruct((filters, MODES), F32),
            ),
            in_specs=[any_spec] * 7,
            out_specs=(vmem_spec,) * 3,
            scratch_shapes=[
                half(rows, chans), wide(tiles, LANES), wide(tiles, LANES), half(rows, chans),
                half(rows, chans), wide(filters, MODES), wide(filters, MODES),
                half(tiles, rows, LANES), half(tiles, rows, LANES),
                wide(tiles, 8, LANES), wide(tiles, 8, LANES),
                half(tiles, 2 * LANES, 2 * LANES), half(tiles, LANES, 2 * LANES),
                wide(plane, 8, LANES), wide(tiles, rows, LANES), wide(PER_TILE, 8, LANES),
                wide(8, LANES), wide(groups, 8, LANES),
                wide(plane, 16, LANES), wide(plane, 16, LANES),
                wide(plane, 16, LANES), wide(plane, 16, LANES),
                wide(plane, 16, LANES), wide(plane, 16, LANES),
                wide(8, LANES), wide(planes, 8, LANES),
                wide(40, LANES), wide(planes, 40, LANES),
                wide(plane, 8, LANES), wide(plane, 8, LANES),
                wide(plane, 16, LANES), wide(plane, 16, LANES),
                wide(plane, 8, LANES),
                pltpu.SemaphoreType.DMA((7,)),
                pltpu.SemaphoreType.DMA((8,)),
                pltpu.SemaphoreType.DMA((8,)),
            ],
            compiler_params=pltpu.CompilerParams(
                collective_id=0, has_side_effects=True, vmem_limit_bytes=48 * 1024 * 1024
            ),
        )(
            features,
            norm_gain.reshape(tiles, LANES),
            skip_gain.reshape(tiles, LANES),
            gate_value,
            cotangent,
            residue,
            log_rate,
        )

    in_specs = (
        P("ctx", "ch"),
        P("ch"),
        P("ch"),
        P("ctx", "ch"),
        P("ctx", "ch"),
        P("ch", None),
        P("ch", None),
    )
    out_specs = (P("ctx", "ch"), P("ch", None), P("ch", None))
    return jax.shard_map(local, mesh=mesh, in_specs=in_specs, out_specs=out_specs, check_vma=False)
```

time: 570 us -> 53.3 us (0.09)
  the two profiles are of different devices: /device:TPU:8 before, /device:TPU:1 now
where the time goes in v1:
time: 53.3 us; the launch traced here: 53 us
  Pallas kernels  46 us (86%)
  local copies, waits for them, and re-layouts  6.36 us (12%)
  between operations  0.67 us (1%)
    pallas_call x1, Pallas kernels, local(): pl.pallas_call(functools.partial(body, plane, planes, groups, rows * bloc...  46 us
    unnamed x15, local copies, waits for them, and re-layouts  5.03 us
    pallas_call x2, local copies, waits for them, and re-layouts, local(): pl.pallas_call(functools.partial(body, plane, planes, groups, rows * bloc...  1.34 us

profile of v1, /device:TPU:1, one launch (start us, length us, event | category | flops | bytes accessed | tf_op | source)
XLA Modules:
  0.0 53.0 jit_solution(4784806973301294123)
XLA Ops:
  0.6 0.0 copy-start.5
  0.6 0.8 %copy.10.res_hbm = f32[64,16]{1,0:T(8,128)S(1)} copy(f32[64,16]{0,1:T(8,128)} %param.12) | data formatting | bytes 8192 | tf_op args[5]
  1.4 0.0 copy-done.5
  1.4 0.0 copy-start.3
  1.4 0.0 copy-start.4
  1.4 0.1 copy.11.lrate_hbm
  1.5 0.6 %copy-done.3 = f32[1024]{0:T(1024)S(1)} copy-done((f32[1024]{0:T(1024)S(1)}, f32[1024]{0:T(1024)}, u32[]{:S(2)}) %copy-start.3) | copy-done | bytes 4120
  2.1 0.0 copy-done.4
  2.1 0.0 copy-start
  2.1 0.9 %copy-done = bf16[128,1024]{1,0:T(8,128)(2,1)S(1)} copy-done((bf16[128,1024]{1,0:T(8,128)(2,1)S(1)}, bf16[128,1024]{1,0:T(8,128)(2,1)}, u32[]{:S(2)}) %copy-start) | copy-done | bytes 262168
  3.1 0.0 copy-start.1
  3.1 0.9 %copy-done.1 = bf16[128,1024]{1,0:T(8,128)(2,1)S(1)} copy-done((bf16[128,1024]{1,0:T(8,128)(2,1)S(1)}, bf16[128,1024]{1,0:T(8,128)(2,1)}, u32[]{:S(2)}) %copy-start.1) | copy-done | bytes 262168
  4.0 0.0 copy-start.2
  4.0 0.9 %copy-done.2 = bf16[128,1024]{1,0:T(8,128)(2,1)S(1)} copy-done((bf16[128,1024]{1,0:T(8,128)(2,1)S(1)}, bf16[128,1024]{1,0:T(8,128)(2,1)}, u32[]{:S(2)}) %copy-start.2) | copy-done | bytes 262168
  5.0 46.0 %shard_map.94 = (bf16[128,1024]{1,0:T(8,128)(2,1)S(1)}, f32[64,16]{1,0:T(8,128)S(1)}, f32[64,16]{1,0:T(8,128)S(1)}) custom-call(bf16[128,1024]{1,0:T(8,128)(2,1)S(1)} %copy-done, f32[8,128]{1,0:T(8,128)S(1)} %bitcast.2, f32[8,128]{1,0:T(8,128)S(1)} %bitcast.3, bf16[128,1024]{1,0:T(8,128)(2,1)S(1)} %copy-done.1, bf16[128,1024]{1,0:T(8,128)(2,1)S(1)} %copy-done.2, ...), custom_call_target="tpu_custom_call" | custom-call | tf_op jit(solution)/shard_map/pallas_call | solution.py:375
  51.0 0.7 %copy.12 = f32[64,16]{0,1:T(8,128)} copy(f32[64,16]{1,0:T(8,128)S(1)} %get-tuple-element.4) | data formatting | bytes 8192 | tf_op jit(solution)/shard_map/pallas_call | solution.py:375
  51.7 0.7 %copy.13 = f32[64,16]{0,1:T(8,128)} copy(f32[64,16]{1,0:T(8,128)S(1)} %get-tuple-element.5) | data formatting | bytes 8192 | tf_op jit(solution)/shard_map/pallas_call | solution.py:375
  52.3 0.7 %copy.15 = bf16[128,1024]{1,0:T(8,128)(2,1)} copy(bf16[128,1024]{1,0:T(8,128)(2,1)S(1)} %get-tuple-element.9) | data formatting | bytes 524288
Async XLA Ops:
  0.6 0.8 %copy-start.5 = (f32[64,16]{0,1:T(8,128)S(1)}, f32[64,16]{0,1:T(8,128)}, u32[]{:S(2)}) copy-start(f32[64,16]{0,1:T(8,128)} %param.13) | copy-start | bytes 12292
  1.4 0.7 %copy-start.3 = (f32[1024]{0:T(1024)S(1)}, f32[1024]{0:T(1024)}, u32[]{:S(2)}) copy-start(f32[1024]{0:T(1024)} %param.8) | copy-start | bytes 12292
  1.4 0.7 %copy-start.4 = (f32[1024]{0:T(1024)S(1)}, f32[1024]{0:T(1024)}, u32[]{:S(2)}) copy-start(f32[1024]{0:T(1024)} %param.9) | copy-start | bytes 12292
  2.1 0.9 %copy-start = (bf16[128,1024]{1,0:T(8,128)(2,1)S(1)}, bf16[128,1024]{1,0:T(8,128)(2,1)}, u32[]{:S(2)}) copy-start(bf16[128,1024]{1,0:T(8,128)(2,1)} %feat_hbm.1) | copy-start | bytes 786436
  3.1 0.9 %copy-start.1 = (bf16[128,1024]{1,0:T(8,128)(2,1)S(1)}, bf16[128,1024]{1,0:T(8,128)(2,1)}, u32[]{:S(2)}) copy-start(bf16[128,1024]{1,0:T(8,128)(2,1)} %gate_hbm.1) | copy-start | bytes 786436
  4.0 0.9 %copy-start.2 = (bf16[128,1024]{1,0:T(8,128)(2,1)S(1)}, bf16[128,1024]{1,0:T(8,128)(2,1)}, u32[]{:S(2)}) copy-start(bf16[128,1024]{1,0:T(8,128)(2,1)} %cot_hbm.1) | copy-start | bytes 786436

commit v2 on v1

v2 whole, which is shorter than its diff:
```python
import functools

import jax
import jax.numpy as jnp
from jax import lax
from jax.experimental import pallas as pl
from jax.experimental.pallas import tpu as pltpu
from jax.sharding import PartitionSpec as P

EPSILON = 1e-06
HIGHEST = lax.Precision.HIGHEST
F32 = jnp.float32
BF16 = jnp.bfloat16
LANES = 128
MODES = 16
GROUP = 16
PER_TILE = 8
SIDE = 4
UNROLL = 8
UNROLL_PAIRS = 8
MESH = pl.DeviceIdType.MESH


def iota(shape, axis):
    return lax.broadcasted_iota(jnp.int32, shape, axis)


def nt(a, b, precision=None):
    return lax.dot_general(
        a, b, (((1,), (1,)), ((), ())), precision=precision, preferred_element_type=F32
    )


def nn(a, b, precision=None):
    return lax.dot_general(
        a, b, (((1,), (0,)), ((), ())), precision=precision, preferred_element_type=F32
    )


def split(x):
    high = x.astype(BF16)
    low = (x - high.astype(F32)).astype(BF16)
    return jnp.concatenate([high, low], axis=1)


def own_filter(values):
    lane_filter = iota((MODES, LANES), 1) // GROUP
    kept = values[:MODES]
    for f in range(1, PER_TILE):
        kept = jnp.where(lane_filter == f, values[f * MODES : (f + 1) * MODES], kept)
    return kept


def body(
    plane, planes, groups, length,
    feat_hbm, gain_hbm, skip_hbm, gate_hbm, cot_hbm, res_hbm, lrate_hbm,
    out_ref, gres_ref, grate_ref,
    feat, gain, skip, gate, cot, res, lrate,
    xn, dn, rate_rows, res_rows, w_sum, a_out, lag_exp, toeplitz, decay, powers, y_local, diag,
    sq_out, sq_in, c_out, c_in, s_out, s_in, l_out, l_in,
    zc_out, zc_in, z_out, z_in, zg_out, zg_in, r_out, r_in, g_out, g_in,
    pre_one,
    load_sem, send_sem, recv_sem, plane_sem, far_sem,
):
    rows = feat.shape[0]
    tiles = feat.shape[1] // LANES
    filters = lrate.shape[1]
    ctx, ch = lax.axis_index("ctx"), lax.axis_index("ch")
    z_me, p_me = ctx // plane, ctx % plane
    x_me, y_me = p_me // SIDE, p_me % SIDE

    loads = [
        pltpu.make_async_copy(src, dst, load_sem.at[n])
        for n, (src, dst) in enumerate(
            (
                (feat_hbm, feat), (lrate_hbm, lrate), (res_hbm, res), (gain_hbm, gain),
                (skip_hbm, skip), (cot_hbm, cot), (gate_hbm, gate),
            )
        )
    ]
    for load in loads:
        load.start()

    def at(z, x, y):
        return {"ctx": z * plane + x * SIDE + y}

    def signal(sem, device):
        pl.semaphore_signal(sem, inc=1, device_id=device, device_id_type=MESH)

    z_next, z_last = (z_me + 1) % planes, (z_me + planes - 1) % planes

    barrier = pltpu.get_barrier_semaphore()
    signal(barrier, at(z_next, x_me, y_me))
    signal(barrier, at(z_last, x_me, y_me))
    for i in (2, 1, 3):
        signal(barrier, at(z_me, (x_me + i) % SIDE, y_me))
        signal(barrier, at(z_me, x_me, (y_me + i) % SIDE))
    for i in range(1, groups):
        signal(barrier, {"ch": (ch + i) % groups})

    def send_plane(src, dst, kind):
        for i in range(1, plane):
            peer = (p_me + i) % plane
            pltpu.make_async_remote_copy(
                src_ref=src.at[peer], dst_ref=dst.at[p_me],
                send_sem=send_sem.at[kind], recv_sem=recv_sem.at[kind],
                device_id={"ctx": z_me * plane + peer}, device_id_type=MESH,
            ).start()

    def send_z(src, dst, kind):
        for i in (2, 1, 3):
            pltpu.make_async_remote_copy(
                src_ref=src, dst_ref=dst.at[z_me],
                send_sem=send_sem.at[kind], recv_sem=recv_sem.at[kind],
                device_id={"ctx": ((z_me + i) % planes) * plane + p_me}, device_id_type=MESH,
            ).start()

    def send_groups(src, dst, kind):
        for i in range(1, groups):
            pltpu.make_async_remote_copy(
                src_ref=src, dst_ref=dst.at[ch],
                send_sem=send_sem.at[kind], recv_sem=recv_sem.at[kind],
                device_id={"ch": (ch + i) % groups}, device_id_type=MESH,
            ).start()

    def wait_in(dst, kind):
        part = dst.at[pl.ds(0, dst.shape[0] - 1)]
        pltpu.make_async_copy(part, part, recv_sem.at[kind]).wait()

    def wait_out(dst, kind):
        part = dst.at[pl.ds(0, dst.shape[0] - 1)]
        pltpu.make_async_copy(part, part, send_sem.at[kind]).wait()

    loads[0].wait()
    squares = jnp.zeros((rows, LANES), F32)
    for j in range(tiles):
        part = feat[:, j * LANES : (j + 1) * LANES].astype(F32)
        squares += part * part
    sq_row = jnp.sum(jnp.transpose(squares), axis=0, keepdims=True)
    sq_out[...] = jnp.broadcast_to(sq_row, sq_out.shape)
    sq_in[ch] = sq_out[...]
    pl.semaphore_wait(barrier, (groups - 1) + 2 * (SIDE - 1) + 2)
    send_groups(sq_out, sq_in, 0)
    for i in range(1, SIDE):
        signal(plane_sem, at(z_me, (x_me + i) % SIDE, y_me))
    signal(far_sem, at(z_last, x_me, y_me))

    loads[1].wait()
    loads[2].wait()
    same_filter = iota((PER_TILE, LANES), 1) // MODES == iota((PER_TILE, LANES), 0)
    lane_mode = iota((MODES, LANES), 1) % MODES == iota((MODES, LANES), 0)
    own_lanes = (
        iota((filters, tiles * LANES), 1) // GROUP == iota((filters, tiles * LANES), 0)
    ).astype(F32)
    spread = nn(jnp.concatenate([jnp.exp(lrate[...]), res[...]], axis=0), own_lanes, HIGHEST)
    for j in range(tiles):
        rate_rep = spread[:MODES, j * LANES : (j + 1) * LANES]
        res_rep = spread[MODES:, j * LANES : (j + 1) * LANES]
        whole = jnp.exp(-rate_rep * float(rows))
        decay[2 * j] = whole[:8]
        decay[2 * j + 1] = whole[8:]
        rate_row = jnp.sum(jnp.where(lane_mode, rate_rep, 0.0), axis=0, keepdims=True)
        res_row = jnp.sum(jnp.where(lane_mode, res_rep, 0.0), axis=0, keepdims=True)
        rate_rows[j] = jnp.broadcast_to(rate_row, (PER_TILE, LANES))
        res_rows[j] = jnp.where(same_filter, res_row, 0.0)
    step = decay[p_me]
    power = jnp.ones((8, LANES), F32)
    for p in range(plane):
        powers[p] = power
        power = power * step
    plane_step = power

    for n in range(3, 7):
        loads[n].wait()
    lane_up = iota((LANES, LANES), 1).astype(F32)
    row_up = iota((LANES, LANES), 0).astype(F32)
    lag_rows = jnp.where(row_up == 0.0, 0.0, rows - row_up)

    def tables(j, carry):
        cols = pl.ds(pl.multiple_of(j * LANES, LANES), LANES)
        rate_wide = jnp.broadcast_to(rate_rows[j, 0:1, :], (LANES, LANES))
        rate_tall = jnp.transpose(rate_wide)
        d_part = (cot[:, cols].astype(F32) * gate[:, cols].astype(F32)).astype(BF16)
        dn[j] = d_part
        ahead = lane_up + 1.0
        after = jnp.exp(-rate_tall * ahead)
        both = jnp.concatenate([split(after), split(after * ahead)], axis=0)
        sums = nn(both, jnp.concatenate([d_part, d_part], axis=0))
        one, two = own_filter(sums[:LANES]), own_filter(sums[LANES:])
        for half in range(2):
            c_out[2 * j + half, 0:8] = one[8 * half : 8 * half + 8]
            c_out[2 * j + half, 8:16] = two[8 * half : 8 * half + 8]
        back = (rows - 1.0) - lane_up
        weight = jnp.exp(-rate_tall * back)
        w_sum[j] = jnp.concatenate([split(weight), split(weight * back)], axis=0)
        return carry

    lax.fori_loop(0, tiles, tables, 0, unroll=UNROLL)
    c_in[p_me] = c_out[p_me]
    pl.semaphore_wait(plane_sem, SIDE - 1)
    send_plane(c_out, c_in, 1)

    tall, wide = iota((2 * MODES // 2, LANES), 0), iota((2 * MODES // 2, LANES), 1)

    def builds(j, carry):
        rate_wide = jnp.broadcast_to(rate_rows[j, 0:1, :], (LANES, LANES))
        res_wide = jnp.sum(res_rows[j], axis=0, keepdims=True)
        leaving = split(res_wide * jnp.exp(-rate_wide * (row_up + 1.0)))
        a_out[j, :, 0 : 2 * LANES] = leaving
        a_out[j, :, 2 * LANES :] = leaving[:, :LANES]
        table = jnp.exp(-rate_wide * lag_rows)
        lag_exp[j] = table
        taps = nt(res_rows[j], table, HIGHEST)
        for f in range(PER_TILE):
            first = pltpu.roll(
                jnp.broadcast_to(taps[f : f + 1], (16, LANES)), 0, 1, stride=1, stride_axis=0
            )
            high = first.astype(BF16)
            low = (first - high.astype(F32)).astype(BF16)
            for i in range(rows // 16):
                causal = wide <= tall + 16 * i
                for side, piece in enumerate((high, low)):
                    moved = pltpu.roll(piece, 16 * i, 1) if i else piece
                    toeplitz[j, f * rows + 16 * i : f * rows + 16 * i + 16, side * LANES : (side + 1) * LANES] = (
                        jnp.where(causal, moved, jnp.zeros_like(moved))
                    )
        return carry

    lax.fori_loop(0, tiles, builds, 0, unroll=UNROLL)

    wait_in(sq_in, 0)
    total_sq = sq_in[0]
    for n in range(1, groups):
        total_sq += sq_in[n]
    inverse = lax.rsqrt(total_sq / float(groups * tiles * LANES) + EPSILON)
    inverse = jnp.transpose(jnp.broadcast_to(inverse[0:1, :], (LANES, LANES)))

    def summaries(j, carry):
        cols = pl.ds(pl.multiple_of(j * LANES, LANES), LANES)
        x_part = (feat[:, cols].astype(F32) * inverse * gain[pl.ds(j, 1), :]).astype(BF16)
        xn[j] = x_part
        sums = nn(w_sum[j], jnp.concatenate([x_part, x_part], axis=0))
        one, two = own_filter(sums[:LANES]), own_filter(sums[LANES:])
        for half in range(2):
            s_out[2 * j + half, 0:8] = one[8 * half : 8 * half + 8]
            s_out[2 * j + half, 8:16] = two[8 * half : 8 * half + 8]
        return carry

    lax.fori_loop(0, tiles, summaries, 0, unroll=UNROLL)
    s_in[p_me] = s_out[p_me]
    send_plane(s_out, s_in, 2)

    wait_in(c_in, 1)
    zero = jnp.zeros((8, LANES), F32)
    back_one, back_two = zero, zero
    for p in range(plane):
        cot_one, cot_two = c_in[p, 0:8], c_in[p, 8:16]
        back_one += powers[p] * cot_one
        back_two += powers[p] * (cot_two + float(rows * p) * cot_one)
    zc_out[0:8] = back_one
    zc_out[8:16] = back_two
    zc_in[z_me] = zc_out[...]
    pl.semaphore_wait(far_sem, 1)
    send_z(zc_out, zc_in, 3)

    lane_filter = iota((rows, LANES), 1) // GROUP
    short_lane, short_row = iota((8, LANES), 1), iota((8, LANES), 0)
    lag_short = jnp.where(short_lane == 0, 0, rows - short_lane).astype(F32)
    in_group = short_lane % GROUP

    def pairs(j, carry):
        x_part, d_part = xn[j], dn[j]
        masked = [
            jnp.where(lane_filter == f, d_part, jnp.zeros_like(d_part)) for f in range(PER_TILE)
        ]
        product = nt(jnp.concatenate(masked, axis=0), x_part)
        for f in range(PER_TILE):
            total = None
            for i in range(rows // 8):
                piece = jnp.where(
                    short_lane <= short_row + 8 * i,
                    product[f * rows + 8 * i : f * rows + 8 * i + 8],
                    0.0,
                )
                if i:
                    piece = pltpu.roll(piece, LANES - 8 * i, 1)
                total = piece if total is None else total + piece
            diag[j, 8 * f : 8 * f + 8] = total
        near = None
        for u in range(8):
            piece = diag[j, pl.ds(u, PER_TILE, stride=8), :]
            if u:
                piece = pltpu.roll(piece, LANES - u, 1)
            near = piece if near is None else near + piece
        stacked = jnp.concatenate([near, near * lag_short], axis=0)
        local = nn(stacked, lag_exp[j], HIGHEST)
        one = jnp.sum(jnp.where(same_filter, local[:8], 0.0), axis=0, keepdims=True)
        two = jnp.sum(jnp.where(same_filter, local[8:], 0.0), axis=0, keepdims=True)
        one = jnp.broadcast_to(one, (8, LANES))
        two = jnp.broadcast_to(two, (8, LANES))
        ones = (one, pltpu.roll(one, LANES - 8, 1))
        twos = (pltpu.roll(two, 8, 1), two)
        for half in range(2):
            l_out[2 * j + half] = jnp.where(
                in_group == short_row, ones[half], jnp.where(in_group == short_row + 8, twos[half], 0.0)
            )
        return carry

    lax.fori_loop(0, tiles, pairs, 0, unroll=UNROLL_PAIRS)
    l_in[p_me] = l_out[p_me]
    send_plane(l_out, l_in, 4)

    wait_in(s_in, 2)
    state = zero
    for p in range(plane):
        pre_one[p] = state
        state = step * state + s_in[p, 0:8]
    z_out[...] = state
    z_in[z_me] = state
    send_z(z_out, z_in, 5)
    second, grad_one, grad_two = zero, zero, zero
    for p in range(plane):
        before = pre_one[p]
        cot_one, cot_two = c_in[p, 0:8], c_in[p, 8:16]
        grad_one += before * cot_one
        grad_two += before * cot_two + second * cot_one
        second = step * (second + float(rows) * before) + s_in[p, 8:16]
    wait_in(zc_in, 3)
    back_one, back_two = zero, zero
    for z in range(planes - 1, 0, -1):
        later = z_me < z
        back_two = jnp.where(
            later, plane_step * (back_two + float(rows * plane) * back_one) + zc_in[z, 8:16], back_two
        )
        back_one = jnp.where(later, plane_step * back_one + zc_in[z, 0:8], back_one)
    grad_one += state * back_one
    grad_two += second * back_one + state * back_two
    first_half = in_group < 8
    packed = jnp.where(
        first_half, grad_one + pltpu.roll(grad_one, LANES - 8, 1), grad_two + pltpu.roll(grad_two, 8, 1)
    )
    wait_in(l_in, 4)
    for p in range(plane):
        packed += l_in[p]
    zg_out[...] = packed
    zg_in[z_me] = packed
    send_z(zg_out, zg_in, 6)

    def inside(j, carry):
        x_part = xn[j]
        spread_out = nn(toeplitz[j], jnp.concatenate([x_part, x_part], axis=0))
        total = spread_out[:rows]
        for f in range(1, PER_TILE):
            total = jnp.where(lane_filter == f, spread_out[f * rows : (f + 1) * rows], total)
        y_local[j] = total + skip[pl.ds(j, 1), :] * x_part.astype(F32)
        return carry

    lax.fori_loop(0, tiles, inside, 0, unroll=UNROLL)

    wait_in(z_in, 5)
    entering = zero
    for z in range(planes - 1):
        entering = jnp.where(z_me > z, plane_step * entering + z_in[z], entering)
    for p in range(plane):
        r_out[p] = pre_one[p] + powers[p] * entering
    r_in[p_me] = r_out[p_me]
    send_plane(r_out, r_in, 7)
    wait_in(zg_in, 6)
    packed = zg_in[0]
    for z in range(1, planes):
        packed += zg_in[z]
    for p in range(plane):
        g_out[p] = packed
    g_in[p_me] = packed
    send_plane(g_out, g_in, 8)

    own = iota((MODES, LANES), 1) // GROUP
    wait_in(r_in, 7)

    def finish(j, carry):
        cols = pl.ds(pl.multiple_of(j * LANES, LANES), LANES)
        states = jnp.concatenate([r_in[2 * j], r_in[2 * j + 1]], axis=0)
        high = states.astype(BF16)
        low = (states - high.astype(F32)).astype(BF16)
        high = [jnp.where(own == f, high, jnp.zeros_like(high)) for f in range(PER_TILE)]
        low = [jnp.where(own == f, low, jnp.zeros_like(low)) for f in range(PER_TILE)]
        carried = nn(a_out[j], jnp.concatenate(high + high + low, axis=0))
        conv = (y_local[j] + carried).astype(BF16)
        out_ref[:, cols] = (gate[:, cols].astype(F32) * conv.astype(F32)).astype(BF16)
        return carry

    lax.fori_loop(0, tiles, finish, 0, unroll=UNROLL)

    wait_in(g_in, 8)
    total = jnp.concatenate(
        [jnp.concatenate([g_in[2 * j], g_in[2 * j + 1]], axis=0) for j in range(tiles)], axis=1
    )
    first_half = iota(total.shape, 1) % GROUP < 8
    total = jnp.concatenate(
        [jnp.where(first_half, total, 0.0), jnp.where(first_half, 0.0, total)], axis=0
    )
    grads = nt(total, own_lanes, HIGHEST)
    gres_ref[...] = grads[:MODES] / float(length)
    grate_ref[...] = -(res[...] * jnp.exp(lrate[...]) / float(length)) * grads[MODES:]

    for kind, buffer in enumerate((sq_in, c_in, s_in, zc_in, l_in, z_in, zg_in, r_in, g_in)):
        wait_out(buffer, kind)


def hand_on(gated, grad_res, grad_rate, gated_hbm, grad_res_hbm, grad_rate_hbm, sem):
    copies = [
        pltpu.make_async_copy(src, dst, sem.at[n])
        for n, (src, dst) in enumerate(
            ((gated, gated_hbm), (grad_res, grad_res_hbm), (grad_rate, grad_rate_hbm))
        )
    ]
    for copy in copies:
        copy.start()
    for copy in copies:
        copy.wait()


def solution(mesh):
    groups = mesh.shape["ch"]
    blocks = mesh.shape["ctx"]
    plane = SIDE * SIDE
    planes = blocks // plane

    def local(features, norm_gain, skip_gain, gate_value, cotangent, residue, log_rate):
        rows, chans = features.shape
        tiles = chans // LANES
        filters = residue.shape[0]
        wide = lambda *shape: pltpu.VMEM(shape, F32)
        half = lambda *shape: pltpu.VMEM(shape, BF16)
        far_spec = pl.BlockSpec(memory_space=pltpu.HBM)
        near_spec = pl.BlockSpec(memory_space=pltpu.VMEM)
        shapes = (
            jax.ShapeDtypeStruct((rows, chans), BF16),
            jax.ShapeDtypeStruct((MODES, filters), F32),
            jax.ShapeDtypeStruct((MODES, filters), F32),
        )
        results = pl.pallas_call(
            functools.partial(body, plane, planes, groups, rows * blocks),
            out_shape=tuple(pltpu.VMEM(part.shape, part.dtype) for part in shapes),
            in_specs=[far_spec] * 7,
            out_specs=(near_spec,) * 3,
            scratch_shapes=[
                half(rows, chans), wide(tiles, LANES), wide(tiles, LANES), half(rows, chans),
                half(rows, chans), wide(MODES, filters), wide(MODES, filters),
                half(tiles, rows, LANES), half(tiles, rows, LANES),
                wide(tiles, 8, LANES), wide(tiles, 8, LANES),
                half(tiles, 2 * LANES, 2 * LANES), half(tiles, LANES, 3 * LANES),
                wide(tiles, rows, LANES), half(tiles, PER_TILE * rows, 2 * LANES),
                wide(plane, 8, LANES), wide(plane, 8, LANES), wide(tiles, rows, LANES),
                wide(tiles, 8 * PER_TILE, LANES),
                wide(8, LANES), wide(groups, 8, LANES),
                wide(plane, 16, LANES), wide(plane, 16, LANES),
                wide(plane, 16, LANES), wide(plane, 16, LANES),
                wide(plane, 8, LANES), wide(plane, 8, LANES),
                wide(16, LANES), wide(planes, 16, LANES),
                wide(8, LANES), wide(planes, 8, LANES),
                wide(8, LANES), wide(planes, 8, LANES),
                wide(plane, 8, LANES), wide(plane, 8, LANES),
                wide(plane, 8, LANES), wide(plane, 8, LANES),
                wide(plane, 8, LANES),
                pltpu.SemaphoreType.DMA((7,)),
                pltpu.SemaphoreType.DMA((9,)),
                pltpu.SemaphoreType.DMA((9,)),
                pltpu.SemaphoreType.REGULAR,
                pltpu.SemaphoreType.REGULAR,
            ],
            compiler_params=pltpu.CompilerParams(
                collective_id=0, has_side_effects=True, vmem_limit_bytes=40 * 1024 * 1024
            ),
        )(
            *(
                pltpu.with_memory_space_constraint(part, pltpu.HBM)
                for part in (
                    features,
                    norm_gain.reshape(tiles, LANES),
                    skip_gain.reshape(tiles, LANES),
                    gate_value,
                    cotangent,
                    residue.T,
                    log_rate.T,
                )
            )
        )
        gated, grad_res, grad_rate = pl.pallas_call(
            hand_on,
            out_shape=tuple(pltpu.HBM(part.shape, part.dtype) for part in shapes),
            in_specs=[near_spec] * 3,
            out_specs=(far_spec,) * 3,
            scratch_shapes=[pltpu.SemaphoreType.DMA((3,))],
        )(*(pltpu.with_memory_space_constraint(part, pltpu.VMEM) for part in results))
        return gated, grad_res.T, grad_rate.T

    in_specs = (
        P("ctx", "ch"),
        P("ch"),
        P("ch"),
        P("ctx", "ch"),
        P("ctx", "ch"),
        P("ch", None),
        P("ch", None),
    )
    out_specs = (P("ctx", "ch"), P("ch", None), P("ch", None))
    return jax.shard_map(local, mesh=mesh, in_specs=in_specs, out_specs=out_specs, check_vma=False)
```

time: 53.3 us -> 43 us (0.81)
  the two profiles are of different devices: /device:TPU:1 before, /device:TPU:4 now
where the time goes in v2:
time: 43 us; the launch traced here: 42.8 us
  Pallas kernels  42.2 us (98%)
  between operations  0.64 us (1%)
    pallas_call x1, Pallas kernels, local(): pl.pallas_call(functools.partial(body, plane, planes, groups, rows * bloc...  41.5 us

profile of v2, /device:TPU:4, one launch (start us, length us, event | category | flops | bytes accessed | tf_op | source)
XLA Modules:
  0.0 42.8 jit_solution(1248560288454402269)
XLA Ops:
  0.6 41.5 %shard_map.94 = (bf16[128,1024]{1,0:T(8,128)(2,1)S(1)}, f32[16,64]{1,0:T(8,128)S(1)}, f32[16,64]{1,0:T(8,128)S(1)}) custom-call(bf16[128,1024]{1,0:T(8,128)(2,1)} %feat_hbm.1, f32[8,128]{1,0:T(8,128)} %bitcast.8, f32[8,128]{1,0:T(8,128)} %bitcast.9, bf16[128,1024]{1,0:T(8,128)(2,1)} %gate_hbm.1, bf16[128,1024]{1,0:T(8,128)(2,1)} %cot_hbm.1, ...), custom_call_target="tpu_custom_call" | custom-call | tf_op jit(solution)/shard_map/pallas_call | solution.py:442
  42.1 0.7 %shard_map.95 = (bf16[128,1024]{1,0:T(8,128)(2,1)}, f32[16,64]{1,0:T(8,128)}, f32[16,64]{1,0:T(8,128)}) custom-call(bf16[128,1024]{1,0:T(8,128)(2,1)S(1)} %get-tuple-element.9.gated, f32[16,64]{1,0:T(8,128)S(1)} %get-tuple-element.10.grad_res, f32[16,64]{1,0:T(8,128)S(1)} %get-tuple-element.11.grad_rate), custom_call_target="tpu_custom_call" | custom-call | tf_op jit(solution)/shard_map/pallas_call | solution.py:489

commit v3 on v2

--- a/solution.py
+++ b/solution.py
@@ -18,6 +18,8 @@
 SIDE = 4
 UNROLL = 8
 UNROLL_PAIRS = 8
+STEP = 16
+CUTS = 4
 MESH = pl.DeviceIdType.MESH
 
 
@@ -57,8 +59,8 @@
     out_ref, gres_ref, grate_ref,
     feat, gain, skip, gate, cot, res, lrate,
     xn, dn, rate_rows, res_rows, w_sum, a_out, lag_exp, toeplitz, decay, powers, y_local, diag,
-    sq_out, sq_in, c_out, c_in, s_out, s_in, l_out, l_in,
-    zc_out, zc_in, z_out, z_in, zg_out, zg_in, r_out, r_in, g_out, g_in,
+    sq_out, sq_in, c_out, c_in, s_out, s_in, ly_out, ly_in, lx_out, lx_in, lz_out, lz_in,
+    z_out, z_in, zg_out, zg_in, r_out, r_in, g_out, g_in,
     pre_one,
     load_sem, send_sem, recv_sem, plane_sem, far_sem,
 ):
@@ -69,16 +71,21 @@
     z_me, p_me = ctx // plane, ctx % plane
     x_me, y_me = p_me // SIDE, p_me % SIDE
 
-    loads = [
+    cut = rows // CUTS
+    small = [
         pltpu.make_async_copy(src, dst, load_sem.at[n])
-        for n, (src, dst) in enumerate(
-            (
-                (feat_hbm, feat), (lrate_hbm, lrate), (res_hbm, res), (gain_hbm, gain),
-                (skip_hbm, skip), (cot_hbm, cot), (gate_hbm, gate),
+        for n, (src, dst) in enumerate(((lrate_hbm, lrate), (res_hbm, res), (gain_hbm, gain), (skip_hbm, skip)))
+    ]
+    large = [
+        [
+            pltpu.make_async_copy(
+                src.at[pl.ds(cut * k, cut)], dst.at[pl.ds(cut * k, cut)], load_sem.at[4 + CUTS * n + k]
             )
-        )
+            for k in range(CUTS)
+        ]
+        for n, (src, dst) in enumerate(((feat_hbm, feat), (cot_hbm, cot), (gate_hbm, gate)))
     ]
-    for load in loads:
+    for load in large[0] + small + large[1] + large[2]:
         load.start()
 
     def at(z, x, y):
@@ -107,13 +114,16 @@
                 device_id={"ctx": z_me * plane + peer}, device_id_type=MESH,
             ).start()
 
-    def send_z(src, dst, kind):
+    def send_line(src, dst, kind, slot, peer):
         for i in (2, 1, 3):
             pltpu.make_async_remote_copy(
-                src_ref=src, dst_ref=dst.at[z_me],
+                src_ref=src, dst_ref=dst.at[slot],
                 send_sem=send_sem.at[kind], recv_sem=recv_sem.at[kind],
-                device_id={"ctx": ((z_me + i) % planes) * plane + p_me}, device_id_type=MESH,
+                device_id=peer(i), device_id_type=MESH,
             ).start()
+
+    def send_z(src, dst, kind):
+        send_line(src, dst, kind, z_me, lambda i: at((z_me + i) % planes, x_me, y_me))
 
     def send_groups(src, dst, kind):
         for i in range(1, groups):
@@ -131,7 +141,8 @@
         part = dst.at[pl.ds(0, dst.shape[0] - 1)]
         pltpu.make_async_copy(part, part, send_sem.at[kind]).wait()
 
-    loads[0].wait()
+    for load in large[0]:
+        load.wait()
     squares = jnp.zeros((rows, LANES), F32)
     for j in range(tiles):
         part = feat[:, j * LANES : (j + 1) * LANES].astype(F32)
@@ -139,14 +150,9 @@
     sq_row = jnp.sum(jnp.transpose(squares), axis=0, keepdims=True)
     sq_out[...] = jnp.broadcast_to(sq_row, sq_out.shape)
     sq_in[ch] = sq_out[...]
-    pl.semaphore_wait(barrier, (groups - 1) + 2 * (SIDE - 1) + 2)
-    send_groups(sq_out, sq_in, 0)
-    for i in range(1, SIDE):
-        signal(plane_sem, at(z_me, (x_me + i) % SIDE, y_me))
-    signal(far_sem, at(z_last, x_me, y_me))
-
-    loads[1].wait()
-    loads[2].wait()
+
+    for load in small:
+        load.wait()
     same_filter = iota((PER_TILE, LANES), 1) // MODES == iota((PER_TILE, LANES), 0)
     lane_mode = iota((MODES, LANES), 1) % MODES == iota((MODES, LANES), 0)
     own_lanes = (
@@ -170,8 +176,8 @@
         power = power * step
     plane_step = power
 
-    for n in range(3, 7):
-        loads[n].wait()
+    for load in large[1] + large[2]:
+        load.wait()
     lane_up = iota((LANES, LANES), 1).astype(F32)
     row_up = iota((LANES, LANES), 0).astype(F32)
     lag_rows = jnp.where(row_up == 0.0, 0.0, rows - row_up)
@@ -197,8 +203,12 @@
 
     lax.fori_loop(0, tiles, tables, 0, unroll=UNROLL)
     c_in[p_me] = c_out[p_me]
-    pl.semaphore_wait(plane_sem, SIDE - 1)
-    send_plane(c_out, c_in, 1)
+    pl.semaphore_wait(barrier, (groups - 1) + 2 * (SIDE - 1) + 2)
+    send_groups(sq_out, sq_in, 0)
+    for i in range(1, SIDE):
+        signal(plane_sem, at(z_me, (x_me + i) % SIDE, y_me))
+    signal(far_sem, at(z_last, x_me, y_me))
+
 
     tall, wide = iota((2 * MODES // 2, LANES), 0), iota((2 * MODES // 2, LANES), 1)
 
@@ -228,6 +238,9 @@
 
     lax.fori_loop(0, tiles, builds, 0, unroll=UNROLL)
 
+    pl.semaphore_wait(plane_sem, SIDE - 1)
+    send_plane(c_out, c_in, 1)
+
     wait_in(sq_in, 0)
     total_sq = sq_in[0]
     for n in range(1, groups):
@@ -250,6 +263,48 @@
     s_in[p_me] = s_out[p_me]
     send_plane(s_out, s_in, 2)
 
+    lane_filter = iota((rows, LANES), 1) // GROUP
+    step_filter = iota((STEP, LANES), 1) // GROUP
+    short_lane, short_row = iota((8, LANES), 1), iota((8, LANES), 0)
+    lag_short = jnp.where(short_lane == 0, 0, rows - short_lane).astype(F32)
+    pair_lane, row_step = iota((PER_TILE * STEP, LANES), 1), iota((PER_TILE * STEP, LANES), 0) % STEP
+    earlier = (pair_lane <= row_step) | (pair_lane >= STEP)
+
+    def pairs(j, carry):
+        x_part, d_part = xn[j], dn[j]
+        left, right = [], []
+        for i in range(rows // STEP):
+            d_rows = d_part[STEP * i : STEP * (i + 1)]
+            left.append(
+                jnp.concatenate(
+                    [jnp.where(step_filter == f, d_rows, jnp.zeros_like(d_rows)) for f in range(PER_TILE)],
+                    axis=0,
+                )
+            )
+            moved = [x_part[STEP * i : STEP * (i + 1)]]
+            if STEP * (i + 1) < rows:
+                moved.append(jnp.zeros((rows - STEP * (i + 1), LANES), BF16))
+            if i:
+                moved.append(x_part[: STEP * i])
+            right.append(jnp.concatenate(moved, axis=0))
+        product = nt(jnp.concatenate(left, axis=1), jnp.concatenate(right, axis=1))
+        diag[j] = jnp.where(earlier, product, 0.0)
+        near = None
+        for u in range(STEP):
+            piece = diag[j, pl.ds(u, PER_TILE, stride=STEP), :]
+            if u:
+                piece = pltpu.roll(piece, LANES - u, 1)
+            near = piece if near is None else near + piece
+        stacked = jnp.concatenate([near, near * lag_short], axis=0)
+        local = nn(stacked, lag_exp[j], HIGHEST)
+        ly_out[pl.ds(j, 1), :] = jnp.sum(jnp.where(same_filter, local[:8], 0.0), axis=0, keepdims=True)
+        ly_out[pl.ds(tiles + j, 1), :] = jnp.sum(jnp.where(same_filter, local[8:], 0.0), axis=0, keepdims=True)
+        return carry
+
+    lax.fori_loop(0, tiles, pairs, 0, unroll=UNROLL_PAIRS)
+    ly_in[y_me] = ly_out[...]
+    send_line(ly_out, ly_in, 3, y_me, lambda i: at(z_me, x_me, (y_me + i) % SIDE))
+
     wait_in(c_in, 1)
     zero = jnp.zeros((8, LANES), F32)
     back_one, back_two = zero, zero
@@ -257,59 +312,9 @@
         cot_one, cot_two = c_in[p, 0:8], c_in[p, 8:16]
         back_one += powers[p] * cot_one
         back_two += powers[p] * (cot_two + float(rows * p) * cot_one)
-    zc_out[0:8] = back_one
-    zc_out[8:16] = back_two
-    zc_in[z_me] = zc_out[...]
+    zg_out[8:16] = back_one
+    zg_out[16:24] = back_two
     pl.semaphore_wait(far_sem, 1)
-    send_z(zc_out, zc_in, 3)
-
-    lane_filter = iota((rows, LANES), 1) // GROUP
-    short_lane, short_row = iota((8, LANES), 1), iota((8, LANES), 0)
-    lag_short = jnp.where(short_lane == 0, 0, rows - short_lane).astype(F32)
-    in_group = short_lane % GROUP
-
-    def pairs(j, carry):
-        x_part, d_part = xn[j], dn[j]
-        masked = [
-            jnp.where(lane_filter == f, d_part, jnp.zeros_like(d_part)) for f in range(PER_TILE)
-        ]
-        product = nt(jnp.concatenate(masked, axis=0), x_part)
-        for f in range(PER_TILE):
-            total = None
-            for i in range(rows // 8):
-                piece = jnp.where(
-                    short_lane <= short_row + 8 * i,
-                    product[f * rows + 8 * i : f * rows + 8 * i + 8],
-                    0.0,
-                )
-                if i:
-                    piece = pltpu.roll(piece, LANES - 8 * i, 1)
-                total = piece if total is None else total + piece
-            diag[j, 8 * f : 8 * f + 8] = total
-        near = None
-        for u in range(8):
-            piece = diag[j, pl.ds(u, PER_TILE, stride=8), :]
-            if u:
-                piece = pltpu.roll(piece, LANES - u, 1)
-            near = piece if near is None else near + piece
-        stacked = jnp.concatenate([near, near * lag_short], axis=0)
-        local = nn(stacked, lag_exp[j], HIGHEST)
-        one = jnp.sum(jnp.where(same_filter, local[:8], 0.0), axis=0, keepdims=True)
-        two = jnp.sum(jnp.where(same_filter, local[8:], 0.0), axis=0, keepdims=True)
-        one = jnp.broadcast_to(one, (8, LANES))
-        two = jnp.broadcast_to(two, (8, LANES))
-        ones = (one, pltpu.roll(one, LANES - 8, 1))
-        twos = (pltpu.roll(two, 8, 1), two)
-        for half in range(2):
-            l_out[2 * j + half] = jnp.where(
-                in_group == short_row, ones[half], jnp.where(in_group == short_row + 8, twos[half], 0.0)
-            )
-        return carry
-
-    lax.fori_loop(0, tiles, pairs, 0, unroll=UNROLL_PAIRS)
-    l_in[p_me] = l_out[p_me]
-    send_plane(l_out, l_in, 4)
-
     wait_in(s_in, 2)
     state = zero
     for p in range(plane):
@@ -317,7 +322,7 @@
         state = step * state + s_in[p, 0:8]
     z_out[...] = state
     z_in[z_me] = state
-    send_z(z_out, z_in, 5)
+    send_z(z_out, z_in, 6)
     second, grad_one, grad_two = zero, zero, zero
     for p in range(plane):
         before = pre_one[p]
@@ -325,26 +330,16 @@
         grad_one += before * cot_one
         grad_two += before * cot_two + second * cot_one
         second = step * (second + float(rows) * before) + s_in[p, 8:16]
-    wait_in(zc_in, 3)
-    back_one, back_two = zero, zero
-    for z in range(planes - 1, 0, -1):
-        later = z_me < z
-        back_two = jnp.where(
-            later, plane_step * (back_two + float(rows * plane) * back_one) + zc_in[z, 8:16], back_two
-        )
-        back_one = jnp.where(later, plane_step * back_one + zc_in[z, 0:8], back_one)
-    grad_one += state * back_one
-    grad_two += second * back_one + state * back_two
-    first_half = in_group < 8
-    packed = jnp.where(
-        first_half, grad_one + pltpu.roll(grad_one, LANES - 8, 1), grad_two + pltpu.roll(grad_two, 8, 1)
-    )
-    wait_in(l_in, 4)
-    for p in range(plane):
-        packed += l_in[p]
-    zg_out[...] = packed
-    zg_in[z_me] = packed
-    send_z(zg_out, zg_in, 6)
+
+    first_half = short_lane % GROUP < GROUP // 2
+
+    def fold(one, two):
+        return jnp.where(first_half, one + pltpu.roll(one, LANES - 8, 1), two + pltpu.roll(two, 8, 1))
+
+    zg_out[0:8] = second
+    zg_out[24:32] = fold(grad_one, grad_two)
+    zg_in[z_me] = zg_out[...]
+    send_z(zg_out, zg_in, 7)
 
     def inside(j, carry):
         x_part = xn[j]
@@ -357,25 +352,40 @@
 
     lax.fori_loop(0, tiles, inside, 0, unroll=UNROLL)
 
-    wait_in(z_in, 5)
+    wait_in(ly_in, 3)
+    lx_out[...] = ((ly_in[0] + ly_in[1]) + ly_in[2]) + ly_in[3]
+    lx_in[x_me] = lx_out[...]
+    send_line(lx_out, lx_in, 4, x_me, lambda i: at(z_me, (x_me + i) % SIDE, y_me))
+
+    wait_in(lx_in, 4)
+    lz_out[...] = ((lx_in[0] + lx_in[1]) + lx_in[2]) + lx_in[3]
+    lz_in[z_me] = lz_out[...]
+    send_z(lz_out, lz_in, 5)
+    wait_in(z_in, 6)
     entering = zero
     for z in range(planes - 1):
         entering = jnp.where(z_me > z, plane_step * entering + z_in[z], entering)
     for p in range(plane):
         r_out[p] = pre_one[p] + powers[p] * entering
     r_in[p_me] = r_out[p_me]
-    send_plane(r_out, r_in, 7)
-    wait_in(zg_in, 6)
-    packed = zg_in[0]
-    for z in range(1, planes):
-        packed += zg_in[z]
+    send_plane(r_out, r_in, 8)
+    wait_in(zg_in, 7)
+    state, second, grad_one, grad_two, packed = zero, zero, zero, zero, zero
+    for z in range(planes):
+        back_one, back_two = zg_in[z, 8:16], zg_in[z, 16:24]
+        grad_one += state * back_one
+        grad_two += second * back_one + state * back_two
+        packed += zg_in[z, 24:32]
+        second = plane_step * (second + float(rows * plane) * state) + zg_in[z, 0:8]
+        state = plane_step * state + z_in[z]
+    packed += fold(grad_one, grad_two)
     for p in range(plane):
         g_out[p] = packed
     g_in[p_me] = packed
-    send_plane(g_out, g_in, 8)
+    send_plane(g_out, g_in, 9)
 
     own = iota((MODES, LANES), 1) // GROUP
-    wait_in(r_in, 7)
+    wait_in(r_in, 8)
 
     def finish(j, carry):
         cols = pl.ds(pl.multiple_of(j * LANES, LANES), LANES)
@@ -391,29 +401,36 @@
 
     lax.fori_loop(0, tiles, finish, 0, unroll=UNROLL)
 
-    wait_in(g_in, 8)
-    total = jnp.concatenate(
-        [jnp.concatenate([g_in[2 * j], g_in[2 * j + 1]], axis=0) for j in range(tiles)], axis=1
-    )
-    first_half = iota(total.shape, 1) % GROUP < 8
-    total = jnp.concatenate(
-        [jnp.where(first_half, total, 0.0), jnp.where(first_half, 0.0, total)], axis=0
-    )
+    wait_in(lz_in, 5)
+    near = ((lz_in[0] + lz_in[1]) + lz_in[2]) + lz_in[3]
+    wait_in(g_in, 9)
+    half_lanes = iota((MODES, LANES), 1) % GROUP < GROUP // 2
+    ones, twos = [], []
+    for j in range(tiles):
+        part = jnp.concatenate([g_in[2 * j], g_in[2 * j + 1]], axis=0)
+        one = jnp.where(lane_mode, near[j : j + 1], 0.0)
+        two = jnp.where(lane_mode, near[tiles + j : tiles + j + 1], 0.0)
+        ones.append(jnp.where(half_lanes, part, 0.0) + one)
+        twos.append(jnp.where(half_lanes, 0.0, part) + two)
+    total = jnp.concatenate([jnp.concatenate(ones, axis=1), jnp.concatenate(twos, axis=1)], axis=0)
     grads = nt(total, own_lanes, HIGHEST)
     gres_ref[...] = grads[:MODES] / float(length)
     grate_ref[...] = -(res[...] * jnp.exp(lrate[...]) / float(length)) * grads[MODES:]
 
-    for kind, buffer in enumerate((sq_in, c_in, s_in, zc_in, l_in, z_in, zg_in, r_in, g_in)):
+    for kind, buffer in enumerate(
+        (sq_in, c_in, s_in, ly_in, lx_in, lz_in, z_in, zg_in, r_in, g_in)
+    ):
         wait_out(buffer, kind)
 
 
 def hand_on(gated, grad_res, grad_rate, gated_hbm, grad_res_hbm, grad_rate_hbm, sem):
+    cut = gated.shape[0] // CUTS
     copies = [
-        pltpu.make_async_copy(src, dst, sem.at[n])
-        for n, (src, dst) in enumerate(
-            ((gated, gated_hbm), (grad_res, grad_res_hbm), (grad_rate, grad_rate_hbm))
-        )
+        pltpu.make_async_copy(gated.at[pl.ds(cut * k, cut)], gated_hbm.at[pl.ds(cut * k, cut)], sem.at[k])
+        for k in range(CUTS)
     ]
+    copies.append(pltpu.make_async_copy(grad_res, grad_res_hbm, sem.at[CUTS]))
+    copies.append(pltpu.make_async_copy(grad_rate, grad_rate_hbm, sem.at[CUTS + 1]))
     for copy in copies:
         copy.start()
     for copy in copies:
@@ -452,20 +469,20 @@
                 half(tiles, 2 * LANES, 2 * LANES), half(tiles, LANES, 3 * LANES),
                 wide(tiles, rows, LANES), half(tiles, PER_TILE * rows, 2 * LANES),
                 wide(plane, 8, LANES), wide(plane, 8, LANES), wide(tiles, rows, LANES),
-                wide(tiles, 8 * PER_TILE, LANES),
+                wide(tiles, STEP * PER_TILE, LANES),
                 wide(8, LANES), wide(groups, 8, LANES),
                 wide(plane, 16, LANES), wide(plane, 16, LANES),
                 wide(plane, 16, LANES), wide(plane, 16, LANES),
-                wide(plane, 8, LANES), wide(plane, 8, LANES),
+                wide(16, LANES), wide(SIDE, 16, LANES), wide(16, LANES), wide(SIDE, 16, LANES),
                 wide(16, LANES), wide(planes, 16, LANES),
                 wide(8, LANES), wide(planes, 8, LANES),
-                wide(8, LANES), wide(planes, 8, LANES),
+                wide(32, LANES), wide(planes, 32, LANES),
                 wide(plane, 8, LANES), wide(plane, 8, LANES),
                 wide(plane, 8, LANES), wide(plane, 8, LANES),
                 wide(plane, 8, LANES),
-                pltpu.SemaphoreType.DMA((7,)),
-                pltpu.SemaphoreType.DMA((9,)),
-                pltpu.SemaphoreType.DMA((9,)),
+                pltpu.SemaphoreType.DMA((4 + 3 * CUTS,)),
+                pltpu.SemaphoreType.DMA((10,)),
+                pltpu.SemaphoreType.DMA((10,)),
                 pltpu.SemaphoreType.REGULAR,
                 pltpu.SemaphoreType.REGULAR,
             ],
@@ -491,7 +508,7 @@
             out_shape=tuple(pltpu.HBM(part.shape, part.dtype) for part in shapes),
             in_specs=[near_spec] * 3,
             out_specs=(far_spec,) * 3,
-            scratch_shapes=[pltpu.SemaphoreType.DMA((3,))],
+            scratch_shapes=[pltpu.SemaphoreType.DMA((CUTS + 2,))],
         )(*(pltpu.with_memory_space_constraint(part, pltpu.VMEM) for part in results))
         return gated, grad_res.T, grad_rate.T
 

time: 43 us -> 37.5 us (0.87)
  the two profiles are of different devices: /device:TPU:4 before, /device:TPU:8 now
where the time goes in v3:
time: 37.5 us; the launch traced here: 37.4 us
  Pallas kernels  36.7 us (98%)
  between operations  0.64 us (2%)
    pallas_call x1, Pallas kernels, local(): pl.pallas_call(functools.partial(body, plane, planes, groups, rows * bloc...  36 us
    pallas_call x1, Pallas kernels, local(): pl.pallas_call(hand_on, out_shape=tuple((pltpu.HBM(part.shape, part.dtype...  0.75 us

profile of v3, /device:TPU:8, one launch (start us, length us, event | category | flops | bytes accessed | tf_op | source)
XLA Modules:
  0.0 37.4 jit_solution(12320419857439718874)
XLA Ops:
  0.6 36.0 %shard_map.94 = (bf16[128,1024]{1,0:T(8,128)(2,1)S(1)}, f32[16,64]{1,0:T(8,128)S(1)}, f32[16,64]{1,0:T(8,128)S(1)}) custom-call(bf16[128,1024]{1,0:T(8,128)(2,1)} %feat_hbm.1, f32[8,128]{1,0:T(8,128)} %bitcast.8, f32[8,128]{1,0:T(8,128)} %bitcast.9, bf16[128,1024]{1,0:T(8,128)(2,1)} %gate_hbm.1, bf16[128,1024]{1,0:T(8,128)(2,1)} %cot_hbm.1, ...), custom_call_target="tpu_custom_call" | custom-call | tf_op jit(solution)/shard_map/pallas_call | solution.py:459
  36.6 0.8 %shard_map.95 = (bf16[128,1024]{1,0:T(8,128)(2,1)}, f32[16,64]{1,0:T(8,128)}, f32[16,64]{1,0:T(8,128)}) custom-call(bf16[128,1024]{1,0:T(8,128)(2,1)S(1)} %get-tuple-element.9.gated, f32[16,64]{1,0:T(8,128)S(1)} %get-tuple-element.10.grad_res, f32[16,64]{1,0:T(8,128)S(1)} %get-tuple-element.11.grad_rate), custom_call_target="tpu_custom_call" | custom-call | tf_op jit(solution)/shard_map/pallas_call | solution.py:506

commit v4 on v3

--- a/solution.py
+++ b/solution.py
@@ -8,7 +8,6 @@
 from jax.sharding import PartitionSpec as P
 
 EPSILON = 1e-06
-HIGHEST = lax.Precision.HIGHEST
 F32 = jnp.float32
 BF16 = jnp.bfloat16
 LANES = 128
@@ -21,28 +20,40 @@
 STEP = 16
 CUTS = 4
 MESH = pl.DeviceIdType.MESH
+FAR_FIRST = sorted(
+    ((a, b) for a in range(SIDE) for b in range(SIDE) if a or b),
+    key=lambda move: (-sum(min(m, SIDE - m) for m in move), move),
+)
 
 
 def iota(shape, axis):
     return lax.broadcasted_iota(jnp.int32, shape, axis)
 
 
-def nt(a, b, precision=None):
-    return lax.dot_general(
-        a, b, (((1,), (1,)), ((), ())), precision=precision, preferred_element_type=F32
-    )
-
-
-def nn(a, b, precision=None):
-    return lax.dot_general(
-        a, b, (((1,), (0,)), ((), ())), precision=precision, preferred_element_type=F32
-    )
+def nt(a, b):
+    return lax.dot_general(a, b, (((1,), (1,)), ((), ())), preferred_element_type=F32)
+
+
+def nn(a, b):
+    return lax.dot_general(a, b, (((1,), (0,)), ((), ())), preferred_element_type=F32)
 
 
 def split(x):
     high = x.astype(BF16)
     low = (x - high.astype(F32)).astype(BF16)
     return jnp.concatenate([high, low], axis=1)
+
+
+def thirds(x):
+    high = x.astype(BF16)
+    rest = x - high.astype(F32)
+    middle = rest.astype(BF16)
+    return jnp.concatenate([high, middle, (rest - middle.astype(F32)).astype(BF16)], axis=0)
+
+
+def halves(x):
+    high = x.astype(BF16)
+    return jnp.concatenate([high, (x - high.astype(F32)).astype(BF16)], axis=0)
 
 
 def own_filter(values):
@@ -60,8 +71,7 @@
     feat, gain, skip, gate, cot, res, lrate,
     xn, dn, rate_rows, res_rows, w_sum, a_out, lag_exp, toeplitz, decay, powers, y_local, diag,
     sq_out, sq_in, c_out, c_in, s_out, s_in, ly_out, ly_in, lx_out, lx_in, lz_out, lz_in,
-    z_out, z_in, zg_out, zg_in, r_out, r_in, g_out, g_in,
-    pre_one,
+    z_out, z_in, r_out, r_in, q_out, q_in,
     load_sem, send_sem, recv_sem, plane_sem, far_sem,
 ):
     rows = feat.shape[0]
@@ -70,6 +80,31 @@
     ctx, ch = lax.axis_index("ctx"), lax.axis_index("ch")
     z_me, p_me = ctx // plane, ctx % plane
     x_me, y_me = p_me // SIDE, p_me % SIDE
+
+    def at(z, x, y):
+        return {"ctx": z * plane + x * SIDE + y}
+
+    def signal(sem, device):
+        pl.semaphore_signal(sem, inc=1, device_id=device, device_id_type=MESH)
+
+    z_next, z_last = (z_me + 1) % planes, (z_me + planes - 1) % planes
+
+    chip, core = ch // 2, ch % 2
+    chips = groups // 2
+    far = (chips - 1) * (1 - chip // (chips // 2))
+    middle = chips // 2 - chip // (chips // 2)
+    near = chips * (chips - 1) // 2 - chip - far - middle
+    far_groups = [2 * other + (core + k) % 2 for other in (far, middle, near) for k in (0, 1)]
+    far_groups.append(2 * chip + 1 - core)
+
+    barrier = pltpu.get_barrier_semaphore()
+    for group in far_groups:
+        signal(barrier, {"ch": group})
+    signal(barrier, at(z_next, x_me, y_me))
+    signal(barrier, at(z_last, x_me, y_me))
+    for i in (2, 1, 3):
+        signal(barrier, at(z_me, (x_me + i) % SIDE, y_me))
+        signal(barrier, at(z_me, x_me, (y_me + i) % SIDE))
 
     cut = rows // CUTS
     small = [
@@ -88,26 +123,9 @@
     for load in large[0] + small + large[1] + large[2]:
         load.start()
 
-    def at(z, x, y):
-        return {"ctx": z * plane + x * SIDE + y}
-
-    def signal(sem, device):
-        pl.semaphore_signal(sem, inc=1, device_id=device, device_id_type=MESH)
-
-    z_next, z_last = (z_me + 1) % planes, (z_me + planes - 1) % planes
-
-    barrier = pltpu.get_barrier_semaphore()
-    signal(barrier, at(z_next, x_me, y_me))
-    signal(barrier, at(z_last, x_me, y_me))
-    for i in (2, 1, 3):
-        signal(barrier, at(z_me, (x_me + i) % SIDE, y_me))
-        signal(barrier, at(z_me, x_me, (y_me + i) % SIDE))
-    for i in range(1, groups):
-        signal(barrier, {"ch": (ch + i) % groups})
-
     def send_plane(src, dst, kind):
-        for i in range(1, plane):
-            peer = (p_me + i) % plane
+        for move_x, move_y in FAR_FIRST:
+            peer = (x_me + move_x) % SIDE * SIDE + (y_me + move_y) % SIDE
             pltpu.make_async_remote_copy(
                 src_ref=src.at[peer], dst_ref=dst.at[p_me],
                 send_sem=send_sem.at[kind], recv_sem=recv_sem.at[kind],
@@ -126,11 +144,11 @@
         send_line(src, dst, kind, z_me, lambda i: at((z_me + i) % planes, x_me, y_me))
 
     def send_groups(src, dst, kind):
-        for i in range(1, groups):
+        for group in far_groups:
             pltpu.make_async_remote_copy(
                 src_ref=src, dst_ref=dst.at[ch],
                 send_sem=send_sem.at[kind], recv_sem=recv_sem.at[kind],
-                device_id={"ch": (ch + i) % groups}, device_id_type=MESH,
+                device_id={"ch": group}, device_id_type=MESH,
             ).start()
 
     def wait_in(dst, kind):
@@ -148,8 +166,13 @@
         part = feat[:, j * LANES : (j + 1) * LANES].astype(F32)
         squares += part * part
     sq_row = jnp.sum(jnp.transpose(squares), axis=0, keepdims=True)
-    sq_out[...] = jnp.broadcast_to(sq_row, sq_out.shape)
+    sq_out[...] = sq_row
     sq_in[ch] = sq_out[...]
+    pl.semaphore_wait(barrier, (groups - 1) + 2 * (SIDE - 1) + 2)
+    send_groups(sq_out, sq_in, 0)
+    for i in range(1, SIDE):
+        signal(plane_sem, at(z_me, (x_me + i) % SIDE, y_me))
+    signal(far_sem, at(z_last, x_me, y_me))
 
     for load in small:
         load.wait()
@@ -157,8 +180,9 @@
     lane_mode = iota((MODES, LANES), 1) % MODES == iota((MODES, LANES), 0)
     own_lanes = (
         iota((filters, tiles * LANES), 1) // GROUP == iota((filters, tiles * LANES), 0)
-    ).astype(F32)
-    spread = nn(jnp.concatenate([jnp.exp(lrate[...]), res[...]], axis=0), own_lanes, HIGHEST)
+    ).astype(F32).astype(BF16)
+    spread = nn(thirds(jnp.concatenate([jnp.exp(lrate[...]), res[...]], axis=0)), own_lanes)
+    spread = spread[: 2 * MODES] + spread[2 * MODES : 4 * MODES] + spread[4 * MODES :]
     for j in range(tiles):
         rate_rep = spread[:MODES, j * LANES : (j + 1) * LANES]
         res_rep = spread[MODES:, j * LANES : (j + 1) * LANES]
@@ -199,44 +223,11 @@
         back = (rows - 1.0) - lane_up
         weight = jnp.exp(-rate_tall * back)
         w_sum[j] = jnp.concatenate([split(weight), split(weight * back)], axis=0)
+        lag_exp[j] = halves(jnp.exp(-rate_wide * lag_rows))
         return carry
 
     lax.fori_loop(0, tiles, tables, 0, unroll=UNROLL)
     c_in[p_me] = c_out[p_me]
-    pl.semaphore_wait(barrier, (groups - 1) + 2 * (SIDE - 1) + 2)
-    send_groups(sq_out, sq_in, 0)
-    for i in range(1, SIDE):
-        signal(plane_sem, at(z_me, (x_me + i) % SIDE, y_me))
-    signal(far_sem, at(z_last, x_me, y_me))
-
-
-    tall, wide = iota((2 * MODES // 2, LANES), 0), iota((2 * MODES // 2, LANES), 1)
-
-    def builds(j, carry):
-        rate_wide = jnp.broadcast_to(rate_rows[j, 0:1, :], (LANES, LANES))
-        res_wide = jnp.sum(res_rows[j], axis=0, keepdims=True)
-        leaving = split(res_wide * jnp.exp(-rate_wide * (row_up + 1.0)))
-        a_out[j, :, 0 : 2 * LANES] = leaving
-        a_out[j, :, 2 * LANES :] = leaving[:, :LANES]
-        table = jnp.exp(-rate_wide * lag_rows)
-        lag_exp[j] = table
-        taps = nt(res_rows[j], table, HIGHEST)
-        for f in range(PER_TILE):
-            first = pltpu.roll(
-                jnp.broadcast_to(taps[f : f + 1], (16, LANES)), 0, 1, stride=1, stride_axis=0
-            )
-            high = first.astype(BF16)
-            low = (first - high.astype(F32)).astype(BF16)
-            for i in range(rows // 16):
-                causal = wide <= tall + 16 * i
-                for side, piece in enumerate((high, low)):
-                    moved = pltpu.roll(piece, 16 * i, 1) if i else piece
-                    toeplitz[j, f * rows + 16 * i : f * rows + 16 * i + 16, side * LANES : (side + 1) * LANES] = (
-                        jnp.where(causal, moved, jnp.zeros_like(moved))
-                    )
-        return carry
-
-    lax.fori_loop(0, tiles, builds, 0, unroll=UNROLL)
 
     pl.semaphore_wait(plane_sem, SIDE - 1)
     send_plane(c_out, c_in, 1)
@@ -246,7 +237,7 @@
     for n in range(1, groups):
         total_sq += sq_in[n]
     inverse = lax.rsqrt(total_sq / float(groups * tiles * LANES) + EPSILON)
-    inverse = jnp.transpose(jnp.broadcast_to(inverse[0:1, :], (LANES, LANES)))
+    inverse = jnp.transpose(jnp.broadcast_to(inverse, (LANES, LANES)))
 
     def summaries(j, carry):
         cols = pl.ds(pl.multiple_of(j * LANES, LANES), LANES)
@@ -296,7 +287,9 @@
                 piece = pltpu.roll(piece, LANES - u, 1)
             near = piece if near is None else near + piece
         stacked = jnp.concatenate([near, near * lag_short], axis=0)
-        local = nn(stacked, lag_exp[j], HIGHEST)
+        stacked = halves(stacked)
+        local = nn(stacked, lag_exp[j, :LANES])
+        local = local[:16] + local[16:] + nn(stacked[:16], lag_exp[j, LANES:])
         ly_out[pl.ds(j, 1), :] = jnp.sum(jnp.where(same_filter, local[:8], 0.0), axis=0, keepdims=True)
         ly_out[pl.ds(tiles + j, 1), :] = jnp.sum(jnp.where(same_filter, local[8:], 0.0), axis=0, keepdims=True)
         return carry
@@ -312,34 +305,65 @@
         cot_one, cot_two = c_in[p, 0:8], c_in[p, 8:16]
         back_one += powers[p] * cot_one
         back_two += powers[p] * (cot_two + float(rows * p) * cot_one)
-    zg_out[8:16] = back_one
-    zg_out[16:24] = back_two
+    z_out[8:16] = back_one
+    z_out[16:24] = back_two
     pl.semaphore_wait(far_sem, 1)
-    wait_in(s_in, 2)
-    state = zero
-    for p in range(plane):
-        pre_one[p] = state
-        state = step * state + s_in[p, 0:8]
-    z_out[...] = state
-    z_in[z_me] = state
-    send_z(z_out, z_in, 6)
-    second, grad_one, grad_two = zero, zero, zero
-    for p in range(plane):
-        before = pre_one[p]
-        cot_one, cot_two = c_in[p, 0:8], c_in[p, 8:16]
-        grad_one += before * cot_one
-        grad_two += before * cot_two + second * cot_one
-        second = step * (second + float(rows) * before) + s_in[p, 8:16]
 
     first_half = short_lane % GROUP < GROUP // 2
 
     def fold(one, two):
         return jnp.where(first_half, one + pltpu.roll(one, LANES - 8, 1), two + pltpu.roll(two, 8, 1))
 
-    zg_out[0:8] = second
-    zg_out[24:32] = fold(grad_one, grad_two)
-    zg_in[z_me] = zg_out[...]
-    send_z(zg_out, zg_in, 7)
+    wait_in(s_in, 2)
+    state, second, grad_one, grad_two = zero, zero, zero, zero
+    for p in range(plane):
+        cot_one, cot_two = c_in[p, 0:8], c_in[p, 8:16]
+        q_out[p] = state
+        grad_one += state * cot_one
+        grad_two += state * cot_two + second * cot_one
+        second = step * (second + float(rows) * state) + s_in[p, 8:16]
+        state = step * state + s_in[p, 0:8]
+    z_out[0:8] = second
+    z_out[24:32] = fold(grad_one, grad_two)
+    z_out[32:40] = state
+    z_in[z_me] = z_out[...]
+    send_z(z_out, z_in, 6)
+    q_in[p_me] = q_out[p_me]
+    send_plane(q_out, q_in, 8)
+
+    wait_in(ly_in, 3)
+    lx_out[...] = ((ly_in[0] + ly_in[1]) + ly_in[2]) + ly_in[3]
+    lx_in[x_me] = lx_out[...]
+    send_line(lx_out, lx_in, 4, x_me, lambda i: at(z_me, (x_me + i) % SIDE, y_me))
+
+    tall, wide = iota((2 * MODES // 2, LANES), 0), iota((2 * MODES // 2, LANES), 1)
+
+    def builds(j, carry):
+        rate_wide = jnp.broadcast_to(rate_rows[j, 0:1, :], (LANES, LANES))
+        res_wide = jnp.sum(res_rows[j], axis=0, keepdims=True)
+        leaving = split(res_wide * jnp.exp(-rate_wide * (row_up + 1.0)))
+        a_out[j, :, 0 : 2 * LANES] = leaving
+        a_out[j, :, 2 * LANES :] = leaving[:, :LANES]
+        table = lag_exp[j]
+        left = halves(res_rows[j])
+        taps = nt(left, table[:LANES])
+        taps = taps[:PER_TILE] + taps[PER_TILE:] + nt(left, table[LANES:])[:PER_TILE]
+        for f in range(PER_TILE):
+            first = pltpu.roll(
+                jnp.broadcast_to(taps[f : f + 1], (16, LANES)), 0, 1, stride=1, stride_axis=0
+            )
+            high = first.astype(BF16)
+            low = (first - high.astype(F32)).astype(BF16)
+            for i in range(rows // 16):
+                causal = wide <= tall + 16 * i
+                for side, piece in enumerate((high, low)):
+                    moved = pltpu.roll(piece, 16 * i, 1) if i else piece
+                    toeplitz[j, f * rows + 16 * i : f * rows + 16 * i + 16, side * LANES : (side + 1) * LANES] = (
+                        jnp.where(causal, moved, jnp.zeros_like(moved))
+                    )
+        return carry
+
+    lax.fori_loop(0, tiles, builds, 0, unroll=UNROLL)
 
     def inside(j, carry):
         x_part = xn[j]
@@ -352,73 +376,77 @@
 
     lax.fori_loop(0, tiles, inside, 0, unroll=UNROLL)
 
-    wait_in(ly_in, 3)
-    lx_out[...] = ((ly_in[0] + ly_in[1]) + ly_in[2]) + ly_in[3]
-    lx_in[x_me] = lx_out[...]
-    send_line(lx_out, lx_in, 4, x_me, lambda i: at(z_me, (x_me + i) % SIDE, y_me))
+    own = iota((MODES, LANES), 1) // GROUP
+
+    def carry_in(source, j, carry):
+        states = jnp.concatenate([source[2 * j, 0:8], source[2 * j + 1, 0:8]], axis=0)
+        high = states.astype(BF16)
+        low = (states - high.astype(F32)).astype(BF16)
+        high = [jnp.where(own == f, high, jnp.zeros_like(high)) for f in range(PER_TILE)]
+        low = [jnp.where(own == f, low, jnp.zeros_like(low)) for f in range(PER_TILE)]
+        y_local[j] += nn(a_out[j], jnp.concatenate(high + high + low, axis=0))
+        return carry
+
+    def finish(j, carry):
+        cols = pl.ds(pl.multiple_of(j * LANES, LANES), LANES)
+        conv = y_local[j].astype(BF16)
+        out_ref[:, cols] = (gate[:, cols].astype(F32) * conv.astype(F32)).astype(BF16)
+        return carry
 
     wait_in(lx_in, 4)
     lz_out[...] = ((lx_in[0] + lx_in[1]) + lx_in[2]) + lx_in[3]
     lz_in[z_me] = lz_out[...]
     send_z(lz_out, lz_in, 5)
+    wait_in(q_in, 8)
+    lax.fori_loop(0, tiles, functools.partial(carry_in, q_in), 0, unroll=UNROLL)
+
+    @pl.when(z_me == 0)
+    def first_plane():
+        lax.fori_loop(0, tiles, finish, 0, unroll=UNROLL)
+
     wait_in(z_in, 6)
     entering = zero
-    for z in range(planes - 1):
-        entering = jnp.where(z_me > z, plane_step * entering + z_in[z], entering)
-    for p in range(plane):
-        r_out[p] = pre_one[p] + powers[p] * entering
-    r_in[p_me] = r_out[p_me]
-    send_plane(r_out, r_in, 8)
-    wait_in(zg_in, 7)
     state, second, grad_one, grad_two, packed = zero, zero, zero, zero, zero
     for z in range(planes):
-        back_one, back_two = zg_in[z, 8:16], zg_in[z, 16:24]
+        back_one, back_two, total_one = z_in[z, 8:16], z_in[z, 16:24], z_in[z, 32:40]
+        entering = jnp.where(z_me == z, state, entering)
         grad_one += state * back_one
         grad_two += second * back_one + state * back_two
-        packed += zg_in[z, 24:32]
-        second = plane_step * (second + float(rows * plane) * state) + zg_in[z, 0:8]
-        state = plane_step * state + z_in[z]
+        packed += z_in[z, 24:32]
+        second = plane_step * (second + float(rows * plane) * state) + z_in[z, 0:8]
+        state = plane_step * state + total_one
     packed += fold(grad_one, grad_two)
     for p in range(plane):
-        g_out[p] = packed
-    g_in[p_me] = packed
-    send_plane(g_out, g_in, 9)
-
-    own = iota((MODES, LANES), 1) // GROUP
-    wait_in(r_in, 8)
-
-    def finish(j, carry):
-        cols = pl.ds(pl.multiple_of(j * LANES, LANES), LANES)
-        states = jnp.concatenate([r_in[2 * j], r_in[2 * j + 1]], axis=0)
-        high = states.astype(BF16)
-        low = (states - high.astype(F32)).astype(BF16)
-        high = [jnp.where(own == f, high, jnp.zeros_like(high)) for f in range(PER_TILE)]
-        low = [jnp.where(own == f, low, jnp.zeros_like(low)) for f in range(PER_TILE)]
-        carried = nn(a_out[j], jnp.concatenate(high + high + low, axis=0))
-        conv = (y_local[j] + carried).astype(BF16)
-        out_ref[:, cols] = (gate[:, cols].astype(F32) * conv.astype(F32)).astype(BF16)
-        return carry
-
-    lax.fori_loop(0, tiles, finish, 0, unroll=UNROLL)
+        r_out[p, 0:8] = powers[p] * entering
+        r_out[p, 8:16] = packed
+    r_in[p_me] = r_out[p_me]
+    send_plane(r_out, r_in, 7)
+
+    wait_in(r_in, 7)
+
+    @pl.when(z_me > 0)
+    def from_other_planes():
+        lax.fori_loop(0, tiles, functools.partial(carry_in, r_in), 0, unroll=UNROLL)
+        lax.fori_loop(0, tiles, finish, 0, unroll=UNROLL)
 
     wait_in(lz_in, 5)
     near = ((lz_in[0] + lz_in[1]) + lz_in[2]) + lz_in[3]
-    wait_in(g_in, 9)
     half_lanes = iota((MODES, LANES), 1) % GROUP < GROUP // 2
     ones, twos = [], []
     for j in range(tiles):
-        part = jnp.concatenate([g_in[2 * j], g_in[2 * j + 1]], axis=0)
+        part = jnp.concatenate([r_in[2 * j, 8:16], r_in[2 * j + 1, 8:16]], axis=0)
         one = jnp.where(lane_mode, near[j : j + 1], 0.0)
         two = jnp.where(lane_mode, near[tiles + j : tiles + j + 1], 0.0)
         ones.append(jnp.where(half_lanes, part, 0.0) + one)
         twos.append(jnp.where(half_lanes, 0.0, part) + two)
     total = jnp.concatenate([jnp.concatenate(ones, axis=1), jnp.concatenate(twos, axis=1)], axis=0)
-    grads = nt(total, own_lanes, HIGHEST)
+    grads = nt(thirds(total), own_lanes)
+    grads = grads[: 2 * MODES] + grads[2 * MODES : 4 * MODES] + grads[4 * MODES :]
     gres_ref[...] = grads[:MODES] / float(length)
     grate_ref[...] = -(res[...] * jnp.exp(lrate[...]) / float(length)) * grads[MODES:]
 
     for kind, buffer in enumerate(
-        (sq_in, c_in, s_in, ly_in, lx_in, lz_in, z_in, zg_in, r_in, g_in)
+        (sq_in, c_in, s_in, ly_in, lx_in, lz_in, z_in, r_in, q_in)
     ):
         wait_out(buffer, kind)
 
@@ -467,22 +495,20 @@
                 half(tiles, rows, LANES), half(tiles, rows, LANES),
                 wide(tiles, 8, LANES), wide(tiles, 8, LANES),
                 half(tiles, 2 * LANES, 2 * LANES), half(tiles, LANES, 3 * LANES),
-                wide(tiles, rows, LANES), half(tiles, PER_TILE * rows, 2 * LANES),
+                half(tiles, 2 * rows, LANES), half(tiles, PER_TILE * rows, 2 * LANES),
                 wide(plane, 8, LANES), wide(plane, 8, LANES), wide(tiles, rows, LANES),
                 wide(tiles, STEP * PER_TILE, LANES),
-                wide(8, LANES), wide(groups, 8, LANES),
+                wide(1, LANES), wide(groups, 1, LANES),
                 wide(plane, 16, LANES), wide(plane, 16, LANES),
                 wide(plane, 16, LANES), wide(plane, 16, LANES),
                 wide(16, LANES), wide(SIDE, 16, LANES), wide(16, LANES), wide(SIDE, 16, LANES),
                 wide(16, LANES), wide(planes, 16, LANES),
-                wide(8, LANES), wide(planes, 8, LANES),
-                wide(32, LANES), wide(planes, 32, LANES),
+                wide(40, LANES), wide(planes, 40, LANES),
+                wide(plane, 16, LANES), wide(plane, 16, LANES),
                 wide(plane, 8, LANES), wide(plane, 8, LANES),
-                wide(plane, 8, LANES), wide(plane, 8, LANES),
-                wide(plane, 8, LANES),
                 pltpu.SemaphoreType.DMA((4 + 3 * CUTS,)),
-                pltpu.SemaphoreType.DMA((10,)),
-                pltpu.SemaphoreType.DMA((10,)),
+                pltpu.SemaphoreType.DMA((9,)),
+                pltpu.SemaphoreType.DMA((9,)),
                 pltpu.SemaphoreType.REGULAR,
                 pltpu.SemaphoreType.REGULAR,
             ],

time: 37.5 us -> 36.7 us (0.979)
  Pallas kernels: 36.7 us -> 35.9 us
    pallas_call x1, Pallas kernels: 36 us -> 35.2 us  [local(): pl.pallas_call(functools.partial(body, plane, planes, groups, rows * bloc...]
where the time goes in v4:
time: 36.7 us; the launch traced here: 36.6 us
  Pallas kernels  35.9 us (98%)
  between operations  0.64 us (2%)
    pallas_call x1, Pallas kernels, local(): pl.pallas_call(functools.partial(body, plane, planes, groups, rows * bloc...  35.2 us
    pallas_call x1, Pallas kernels, local(): pl.pallas_call(hand_on, out_shape=tuple((pltpu.HBM(part.shape, part.dtype...  0.75 us

profile of v4, /device:TPU:8, one launch (start us, length us, event | category | flops | bytes accessed | tf_op | source)
XLA Modules:
  0.0 36.6 jit_solution(11673242966942979068)
XLA Ops:
  0.6 35.2 %shard_map.94 = (bf16[128,1024]{1,0:T(8,128)(2,1)S(1)}, f32[16,64]{1,0:T(8,128)S(1)}, f32[16,64]{1,0:T(8,128)S(1)}) custom-call(bf16[128,1024]{1,0:T(8,128)(2,1)} %feat_hbm.1, f32[8,128]{1,0:T(8,128)} %bitcast.8, f32[8,128]{1,0:T(8,128)} %bitcast.9, bf16[128,1024]{1,0:T(8,128)(2,1)} %gate_hbm.1, bf16[128,1024]{1,0:T(8,128)(2,1)} %cot_hbm.1, ...), custom_call_target="tpu_custom_call" | custom-call | tf_op jit(solution)/shard_map/pallas_call | solution.py:487
  35.8 0.8 %shard_map.95 = (bf16[128,1024]{1,0:T(8,128)(2,1)}, f32[16,64]{1,0:T(8,128)}, f32[16,64]{1,0:T(8,128)}) custom-call(bf16[128,1024]{1,0:T(8,128)(2,1)S(1)} %get-tuple-element.9.gated, f32[16,64]{1,0:T(8,128)S(1)} %get-tuple-element.10.grad_res, f32[16,64]{1,0:T(8,128)S(1)} %get-tuple-element.11.grad_rate), custom_call_target="tpu_custom_call" | custom-call | tf_op jit(solution)/shard_map/pallas_call | solution.py:532

commit v5 on v4

--- a/solution.py
+++ b/solution.py
@@ -98,10 +98,10 @@
     far_groups.append(2 * chip + 1 - core)
 
     barrier = pltpu.get_barrier_semaphore()
+    signal(barrier, at(z_next, x_me, y_me))
+    signal(barrier, at(z_last, x_me, y_me))
     for group in far_groups:
         signal(barrier, {"ch": group})
-    signal(barrier, at(z_next, x_me, y_me))
-    signal(barrier, at(z_last, x_me, y_me))
     for i in (2, 1, 3):
         signal(barrier, at(z_me, (x_me + i) % SIDE, y_me))
         signal(barrier, at(z_me, x_me, (y_me + i) % SIDE))

time: 36.7 us -> 36.7 us (level)
  no operation moved by 1% of the time
where the time goes in v5:
time: 36.7 us; the launch traced here: 36.5 us
  Pallas kernels  35.9 us (98%)
  between operations  0.64 us (2%)
    pallas_call x1, Pallas kernels, local(): pl.pallas_call(functools.partial(body, plane, planes, groups, rows * bloc...  35.1 us
    pallas_call x1, Pallas kernels, local(): pl.pallas_call(hand_on, out_shape=tuple((pltpu.HBM(part.shape, part.dtype...  0.75 us

profile of v5, /device:TPU:8, one launch (start us, length us, event | category | flops | bytes accessed | tf_op | source)
XLA Modules:
  0.0 36.5 jit_solution(13549010198494337533)
XLA Ops:
  0.6 35.1 %shard_map.94 = (bf16[128,1024]{1,0:T(8,128)(2,1)S(1)}, f32[16,64]{1,0:T(8,128)S(1)}, f32[16,64]{1,0:T(8,128)S(1)}) custom-call(bf16[128,1024]{1,0:T(8,128)(2,1)} %feat_hbm.1, f32[8,128]{1,0:T(8,128)} %bitcast.8, f32[8,128]{1,0:T(8,128)} %bitcast.9, bf16[128,1024]{1,0:T(8,128)(2,1)} %gate_hbm.1, bf16[128,1024]{1,0:T(8,128)(2,1)} %cot_hbm.1, ...), custom_call_target="tpu_custom_call" | custom-call | tf_op jit(solution)/shard_map/pallas_call | solution.py:487
  35.8 0.8 %shard_map.95 = (bf16[128,1024]{1,0:T(8,128)(2,1)}, f32[16,64]{1,0:T(8,128)}, f32[16,64]{1,0:T(8,128)}) custom-call(bf16[128,1024]{1,0:T(8,128)(2,1)S(1)} %get-tuple-element.9.gated, f32[16,64]{1,0:T(8,128)S(1)} %get-tuple-element.10.grad_res, f32[16,64]{1,0:T(8,128)S(1)} %get-tuple-element.11.grad_rate), custom_call_target="tpu_custom_call" | custom-call | tf_op jit(solution)/shard_map/pallas_call | solution.py:532
